TPU v7x, 32 devices: a whole 2x2x4 slice. The times are simulated.
32 devices in a mesh: ctx: 16 (over z, y, x), wa: 2 (over core).
Axes of the slice: x: 2, y: 2, z: 4, core: 2. Of those that a mesh axis runs over, the one named last changes fastest.
Arguments:
- hidden_in: bfloat16 [256, 16, 1024], P(None, 'ctx'), may hold values from -6 to 6
- attn_gain: float32 [1024], replicated, may hold values from 0.25 to 1.75
- query_weight: bfloat16 [1024, 1024], P(None, 'wa'), may hold values from -0.1875 to 0.1875
- key_weight: bfloat16 [1024, 512], P(None, 'wa'), may hold values from -0.1875 to 0.1875
- value_weight: bfloat16 [1024, 512], P(None, 'wa'), may hold values from -0.1875 to 0.1875
- query_gain: float32 [64], replicated, may hold values from 0.6 to 1.8
- key_gain: float32 [64], replicated, may hold values from 0.6 to 1.8
- out_weight: bfloat16 [1024, 1024], P('wa'), may hold values from -1.5 to 1.5
- ffn_gain: float32 [1024], replicated, may hold values from 0.25 to 1.75
- gate_weight: bfloat16 [1024, 4608], P(None, 'wa'), may hold values from -0.1875 to 0.1875
- up_weight: bfloat16 [1024, 4608], P(None, 'wa'), may hold values from -0.1875 to 0.1875
- down_weight: bfloat16 [4608, 1024], P('wa'), may hold values from -0.09375 to 0.09375
- query_adapt_in: bfloat16 [1024, 128], replicated, may hold values from -0.1875 to 0.1875
- query_adapt_out: bfloat16 [128, 1024], P(None, 'wa'), may hold values from -0.75 to 0.75
- key_adapt_in: bfloat16 [1024, 128], replicated, may hold values from -0.1875 to 0.1875
- key_adapt_out: bfloat16 [128, 512], P(None, 'wa'), may hold values from -0.75 to 0.75
- value_adapt_in: bfloat16 [1024, 128], replicated, may hold values from -0.1875 to 0.1875
- value_adapt_out: bfloat16 [128, 512], P(None, 'wa'), may hold values from -0.75 to 0.75
- out_adapt_in: bfloat16 [1024, 128], P('wa'), may hold values from -1.5 to 1.5
- out_adapt_out: bfloat16 [128, 1024], replicated, may hold values from -0.75 to 0.75
- gate_adapt_in: bfloat16 [1024, 128], replicated, may hold values from -0.1875 to 0.1875
- gate_adapt_out: bfloat16 [128, 4608], P(None, 'wa'), may hold values from -0.75 to 0.75
- up_adapt_in: bfloat16 [1024, 128], replicated, may hold values from -0.1875 to 0.1875
- up_adapt_out: bfloat16 [128, 4608], P(None, 'wa'), may hold values from -0.75 to 0.75
- down_adapt_in: bfloat16 [4608, 128], P('wa'), may hold values from -0.09375 to 0.09375
- down_adapt_out: bfloat16 [128, 1024], replicated, may hold values from -0.75 to 0.75
- document_extra: int32 [4], replicated, may hold values from 1 to 1801, 3300 in all
- document_adapter: int32 [4], replicated, may hold values from 0 to 7
- cotangent: bfloat16 [256, 16, 1024], P(None, 'ctx'), may hold values from -6 to 6
Outputs:
- output: bfloat16 [256, 16, 1024], P(None, 'ctx')
- input_grad: bfloat16 [256, 16, 1024], P(None, 'ctx')
- query_in_grad: float32 [1024, 128], replicated
- query_out_grad: float32 [128, 1024], P(None, 'wa')
- key_in_grad: float32 [1024, 128], replicated
- key_out_grad: float32 [128, 512], P(None, 'wa')
- value_in_grad: float32 [1024, 128], replicated
- value_out_grad: float32 [128, 512], P(None, 'wa')
- out_in_grad: float32 [1024, 128], P('wa')
- out_out_grad: float32 [128, 1024], replicated
- gate_in_grad: float32 [1024, 128], replicated
- gate_out_grad: float32 [128, 4608], P(None, 'wa')
- up_in_grad: float32 [1024, 128], replicated
- up_out_grad: float32 [128, 4608], P(None, 'wa')
- down_in_grad: float32 [4608, 128], P('wa')
- down_out_grad: float32 [128, 1024], replicated
Inputs may be any that keep to these rules, and one draw needn't show every extreme that they name: Document j has document_extra[j] + 199 tokens; the documents fill the 4096 tokens in order, and one has exactly 2000 tokens.
All inputs are finite; a program needn't handle non-finite values.
Results may differ from a plain program's by a relative error of at most 0.02.
Values may be sent and summed in bfloat16 or wider, within the bound.
No kernel may reach another device: no remote copies, remote signals or barrier semaphores. Data moves between devices by JAX's collectives and lax.ppermute only.
A program may use at most 256 MiB of HBM per device.

v0:
```python
import functools
import math

import jax
import jax.numpy as jnp
import numpy as np
from jax import lax
from jax.experimental import pallas as pl
from jax.experimental.pallas import tpu as pltpu
from jax.sharding import PartitionSpec as P

RANK = 16
DOC_MIN = 200

norm_eps = 1e-05
theta_base = 1000000.0
BF = jnp.bfloat16
F32 = jnp.float32
LOG2E = 1.4426950408889634
STEP, STEP_QUERY = 11, 11
FFN_TILE, FFN_STEP = 256, 3
VMEM_SMALL = 28 * 1024 * 1024
VMEM_LARGE = 56 * 1024 * 1024


def mm(left, right):
    return jnp.dot(left, right, preferred_element_type=F32)


def mm_nt(left, right):
    return lax.dot_general(left, right, (((1,), (1,)), ((), ())), preferred_element_type=F32)


def mm_tn(left, right):
    return lax.dot_general(left, right, (((0,), (0,)), ((), ())), preferred_element_type=F32)


def iota(shape, dim):
    return lax.broadcasted_iota(jnp.int32, shape, dim)


class Cfg:
    def __init__(self, tokens, n_ctx, heads_kv, groups, head_dim, docs, adapt_width, width, hidden):
        self.T = tokens
        self.n = n_ctx
        self.G = heads_kv
        self.lo = n_ctx // heads_kv
        self.groups = groups
        self.hd = head_dim
        self.docs = docs
        self.AW = adapt_width
        self.slots = min(docs, adapt_width // RANK)
        self.S = self.slots * RANK
        self.D = width
        self.F = hidden
        self.R = max(16, min(tokens, 512 // n_ctx))
        self.NT = tokens // self.R
        self.span = self.R * n_ctx
        self.QH = self.G * self.R
        self.KT = n_ctx * self.R


class Meta:
    def __init__(self, extra, adapter, items=None):
        self.refs, self.docs, self.items = (extra, adapter), extra.shape[0], items

    def __getitem__(self, i):
        if i < 2:
            return lax.axis_index(("ctx", "wa")[i])
        return self.refs[(i - 2) // self.docs][(i - 2) % self.docs]


def with_meta(kernel, count):
    return lambda *refs: kernel(Meta(*refs[:count]), *refs[count:])


def doc_starts(cfg, meta):
    out = [jnp.int32(0)]
    for j in range(cfg.docs):
        out.append(out[-1] + meta[2 + j] + (DOC_MIN - 1))
    return out


def start_of(starts, token):
    out = jnp.zeros_like(token)
    for s in starts[1:-1]:
        out = jnp.where(token >= s, s, out)
    return out


def end_of(starts, token):
    out = starts[1]
    for j in range(1, len(starts) - 1):
        out = jnp.where(token >= starts[j], starts[j + 1], out)
    return out


def adapter_mask(cfg, meta):
    token = iota((cfg.T, cfg.AW), 0) * cfg.n + meta[0]
    starts = doc_starts(cfg, meta)
    adapter = jnp.full((cfg.T, cfg.AW), meta[2 + cfg.docs], jnp.int32)
    for j in range(1, cfg.docs):
        adapter = jnp.where(token >= starts[j], meta[2 + cfg.docs + j], adapter)
    return (adapter == iota((cfg.T, cfg.AW), 1) // RANK).astype(F32)


def slot_select(cfg, meta):
    row = iota((cfg.AW, cfg.S), 0)
    col = iota((cfg.AW, cfg.S), 1)
    if cfg.S == cfg.AW:
        return (row == col).astype(BF)
    target = jnp.full((cfg.AW, cfg.S), -1, jnp.int32)
    for s in range(cfg.slots):
        mine = meta[2 + cfg.docs + s]
        again = jnp.int32(0)
        for e in range(s):
            again = jnp.where(meta[2 + cfg.docs + e] == mine, 1, again)
        base = jnp.where(again == 1, -4 * cfg.AW, mine * RANK)
        target = jnp.where(col // RANK == s, base + col % RANK, target)
    return (row == target).astype(BF)


def block_mean(values, hd):
    part = min(values.shape[1], 256)
    ones = (iota((part, part), 0) // hd == iota((part, part), 1) // hd).astype(BF)
    out = []
    for at in range(0, values.shape[1], part):
        piece = values[:, at : at + part]
        high = piece.astype(BF)
        low = (piece - high.astype(F32)).astype(BF)
        out.append((mm(high, ones) + mm(low, ones)) * (1.0 / hd))
    return jnp.concatenate(out, axis=1)


def swap_halves(values, hd):
    width = values.shape[1]
    half = hd // 2
    first = iota(values.shape, 1) % hd < half
    return jnp.where(first, pltpu.roll(values, width - half, 1), pltpu.roll(values, half, 1))


def lanes(values, copies):
    return jnp.concatenate([values] * copies, axis=1) if copies > 1 else values


def params(large=False, **kw):
    limit = VMEM_SMALL if lax.axis_size("ctx") <= 16 and not large else VMEM_LARGE
    return pltpu.CompilerParams(vmem_limit_bytes=limit, **kw)


SMEM = pl.BlockSpec(memory_space=pltpu.SMEM)


def cost(us):
    return pl.CostEstimate(flops=int(us * 1.15e9), bytes_accessed=0, transcendentals=0)


def call(kernel, outs, ins, scratch=(), us=1.0, name=None, large=False, in_place=0, lists=0):
    count = len(ins[0])
    ins = [*ins[0], *ins[1:]]
    return pl.pallas_call(
        with_meta(kernel, count),
        out_shape=[jax.ShapeDtypeStruct(s, d) for s, d in outs],
        in_specs=[SMEM] * count
        + [pl.BlockSpec(memory_space=pl.ANY)] * in_place
        + [pl.BlockSpec(memory_space=pltpu.VMEM)] * (len(ins) - count - in_place),
        out_specs=[pl.BlockSpec(memory_space=pltpu.VMEM)] * (len(outs) - lists) + [SMEM] * lists,
        scratch_shapes=list(scratch),
        compiler_params=params(large),
        cost_estimate=cost(us),
        name=name,
    )(*ins)


def head_prep(cfg, cos, sin, raw, g):
    hd = cfg.hd
    copies = raw.shape[1] // hd
    scaled = raw * lax.rsqrt(block_mean(raw * raw, hd) + norm_eps) * lanes(g[...], copies)
    per = raw.shape[1] // cos.shape[1]
    return scaled * lanes(cos[...], per) + swap_halves(scaled, hd) * lanes(sin[...], per)


def rotation(cfg, meta, inverse, cos, sin):
    width, half = 2 * cfg.hd, cfg.hd // 2
    blocks = width // half
    rows = cfg.T // blocks
    lane = iota((rows, width), 1)
    token = ((lane // half) * rows + iota((rows, width), 0)) * cfg.n + meta[0]
    angle = (token - start_of(doc_starts(cfg, meta), token)).astype(F32) * inverse[...]
    sign = jnp.where(lane % cfg.hd < half, -1.0, 1.0)
    for out, values, scale in ((cos, jnp.cos(angle), None), (sin, jnp.sin(angle), sign)):
        for b in range(blocks):
            part = pltpu.roll(values, width - b * half, 1) if b else values
            part = jnp.where(lane < half, part, 0.0)
            size = half
            while size < width:
                part = part + pltpu.roll(part, size, 1)
                size *= 2
            out[b * rows : (b + 1) * rows, :] = part if scale is None else part * scale


def key_value_kernel(cfg, meta, *refs):
    G, hd = cfg.G, cfg.hd
    sources, (gain, kg, inverse), refs = refs[:7], refs[7:10], refs[10:]
    kv_out, refs = refs[:G], refs[G:]
    raw_ref, sides_ref, normed_ref, cos, sin, *scratch = refs
    buffers, sems, kv_scr = scratch[:7], scratch[7], scratch[8]
    copies = [
        pltpu.make_async_copy(source, buffer, sems.at[i])
        for i, (source, buffer) in enumerate(zip(sources, buffers))
    ]
    for copy in copies:
        copy.start()
    x_buf, ak, av, wk, bk, wv, bv = buffers
    rotation(cfg, meta, inverse, cos, sin)
    mask = adapter_mask(cfg, meta)
    select = slot_select(cfg, meta)
    copies[0].wait()
    x = x_buf[...].astype(F32)
    rr = lax.rsqrt(jnp.mean(x * x, axis=-1, keepdims=True) + norm_eps)
    normed = (x * rr * gain[...]).astype(BF)
    normed_ref[...] = normed
    for copy in copies[1:]:
        copy.wait()
    raws = []
    for i, (w, a, b) in enumerate(((wk, ak, bk), (wv, av, bv))):
        side = (mask * mm(normed, a[...])).astype(BF)
        sides_ref[i] = mm(side, select).astype(BF)
        raws.append(mm(normed, w[...]) + mm(side, b[...]))
    kraw, vraw = raws
    raw_ref[...] = kraw
    key = head_prep(cfg, cos, sin, kraw, kg).astype(BF)
    value = vraw.astype(BF)
    for h in range(G):
        at = slice(h * hd, (h + 1) * hd)
        kv_scr[h] = jnp.concatenate([key[:, at], value[:, at]], axis=1)
    hi = meta[0] // cfg.lo
    for k in range(G):
        kv_out[k][...] = kv_scr[hi ^ k]


def query_kernel(cfg, meta, normed_ref, cos, sin, w, a, b, g, *refs):
    G = cfg.G
    q_out, raw_ref, side_ref, items, q_scr = refs[:G], *refs[G:]
    list_items(cfg, doc_starts(cfg, meta), items)
    normed = normed_ref[...]
    side = (adapter_mask(cfg, meta) * mm(normed, a[...])).astype(BF)
    side_ref[0] = mm(side, slot_select(cfg, meta)).astype(BF)
    raw = mm(normed, w[...]) + mm(side, b[...])
    raw_ref[...] = raw
    query = head_prep(cfg, cos, sin, raw, g).astype(BF)
    gw = cfg.groups * cfg.hd
    for h in range(G):
        q_scr[h] = query[:, h * gw : (h + 1) * gw]
    hi = meta[0] // cfg.lo
    for k in range(G):
        q_out[k][...] = q_scr[hi ^ k]


def tile_of(cfg, pieces, t):
    rows = pl.ds(pl.multiple_of(t * cfg.R, cfg.R), cfg.R)
    return jnp.concatenate([piece[rows, :] for piece in pieces], axis=0)


def list_items(cfg, starts, items):
    def per_query(qt, count):
        def one(s, at):
            items[0, at] = qt
            items[1, at] = s
            return at + 1

        return lax.fori_loop(start_of(starts, qt * cfg.span) // cfg.span, qt + 1, one, count)

    count = lax.fori_loop(0, cfg.NT, per_query, 0)
    for i in range(STEP - 1):
        items[0, count + i] = 0
        items[1, count + i] = cfg.NT - 1
    items[0, items.shape[1] - 1] = count


def steps_of(items, step):
    return (items[0, items.shape[1] - 1] + step - 1) // step


def items_shape(cfg):
    return ((2, cfg.NT * (cfg.NT + 1) // 2 + STEP), jnp.int32)


def split_pieces(ref, count):
    return [ref.at[i] for i in range(count)]


def message_pieces(cfg, ref):
    return [ref.at[pl.ds(k * cfg.T, cfg.T)] for k in range(cfg.G)]


def token_in_span(cfg, meta, index):
    hi, lo = meta[0] // cfg.lo, meta[0] % cfg.lo
    piece, row = index // cfg.R, index % cfg.R
    j, k = piece // cfg.G, piece % cfg.G
    return row * cfg.n + (hi ^ k) * cfg.lo + (lo ^ j)


def pad_queries(cfg, qq, side):
    hd = cfg.hd
    wide = qq.astype(F32)
    first = iota(wide.shape, 1) < hd
    rolled = pltpu.roll(wide, hd, 1)
    if side == 0:
        parts = [jnp.where(first, wide, 0.0), jnp.where(first, rolled, 0.0)]
    else:
        parts = [jnp.where(first, 0.0, rolled), jnp.where(first, 0.0, wide)]
    return jnp.concatenate(parts, axis=0).astype(BF)


def attend_kernel(cfg, meta, *refs):
    G, R, hd, QH = cfg.G, cfg.R, cfg.hd, cfg.QH
    q_in, own, others = refs[:G], refs[G], refs[G + 1 : G + cfg.lo]
    rest = refs[G + cfg.lo :]
    o_out, o_all, linv, q_scr, acc_scr = rest[:G], *rest[G:]
    kv_pieces = split_pieces(own, G)
    for ref in others:
        kv_pieces = kv_pieces + split_pieces(ref, G)
    starts = doc_starts(cfg, meta)
    items = meta.items
    scale = hd ** (-0.5) * LOG2E
    key_off = token_in_span(cfg, meta, iota((1, cfg.KT), 1))
    row_off = token_in_span(cfg, meta, iota((2 * QH, 1), 0) % QH)
    key_lanes = iota((cfg.KT, 2 * hd), 1) < hd
    for t in range(cfg.NT):
        q_scr[t] = pad_queries(cfg, tile_of(cfg, q_in, t), 0)
        acc_scr[t] = jnp.zeros((2 * QH, 2 * hd), F32)

    def step(i, carry):
        parts = []
        for u in range(STEP):
            qt, s = items[0, i * STEP + u], items[1, i * STEP + u]
            kv = tile_of(cfg, kv_pieces, s)
            token = row_off + qt * cfg.span
            key_token = key_off + s * cfg.span
            e = jnp.exp2(mm_nt(q_scr[qt], kv) * scale)
            e = jnp.where((key_token <= token) & (key_token >= start_of(starts, token)), e, 0.0)
            parts.append((qt, mm(e.astype(BF), jnp.where(key_lanes, jnp.ones_like(kv), kv))))
        for qt, part in parts:
            acc_scr[qt] += part
        return carry

    lax.fori_loop(0, steps_of(items, STEP), step, 0)
    half = iota((QH, 2 * hd), 1) < hd
    for t in range(cfg.NT):
        acc = acc_scr[t]
        inv0 = 1.0 / acc[:QH]
        inv1 = 1.0 / acc[QH:]
        out0 = pltpu.roll(acc[:QH], hd, 1) * inv0
        out1 = acc[QH:] * pltpu.roll(inv1, hd, 1)
        out = jnp.where(half, out0, out1).astype(BF)
        inv = jnp.where(half, inv0, pltpu.roll(inv1, hd, 1))
        rows = slice(t * R, (t + 1) * R)
        for k in range(G):
            o_out[k][rows, :] = out[k * R : (k + 1) * R]
            o_all[k, rows, :] = out[k * R : (k + 1) * R]
            linv[k, rows, :] = inv[k * R : (k + 1) * R]


def head_sums(cfg, prod):
    pick = (iota((16, prod.shape[1]), 1) // cfg.hd == iota((16, prod.shape[1]), 0)).astype(BF)
    high = prod.astype(BF)
    low = (prod - high.astype(F32)).astype(BF)
    return mm_nt(pick, high) + mm_nt(pick, low)


def scale_kernel(cfg, meta, *refs):
    G, T, R, NT, QH = cfg.G, cfg.T, cfg.R, cfg.NT, cfg.QH
    go, linv, o_all, out, scr, delta = refs[:G], refs[G], refs[G + 1], refs[G + 2], *refs[G + 3 :]
    delta[...] = jnp.zeros_like(delta)
    for k in range(G):
        scaled = (go[k][...].astype(F32) * linv[k]).astype(BF)
        out[k * T : (k + 1) * T, :] = scaled
        prod = scaled.astype(F32) * o_all[k].astype(F32)
        for t in range(NT):
            scr[t, k * R : (k + 1) * R, :] = prod[t * R : (t + 1) * R]
    for t in range(NT):
        sums = head_sums(cfg, scr[t])
        for h in range(cfg.groups):
            delta[h * NT + t : h * NT + t + 1, :QH] = sums[h : h + 1]
    high = delta[...].astype(BF)
    at = G * T
    rows = cfg.groups * NT
    out[at : at + rows, :] = high
    out[at + rows : at + 2 * rows, :] = (delta[...] - high.astype(F32)).astype(BF)


def grad_query_kernel(cfg, meta, *refs):
    G, R, hd, QH = cfg.G, cfg.R, cfg.hd, cfg.QH
    q_in, own, others = refs[:G], refs[G], refs[G + 1 : G + cfg.lo]
    go_ref, o_ref = refs[G + cfg.lo : G + cfg.lo + 2]
    rest = refs[G + cfg.lo + 2 :]
    dq_out, q_scr, go_scr, delta_scr, acc_scr = rest[:G], *rest[G:]
    kv_pieces = split_pieces(own, G)
    for ref in others:
        kv_pieces = kv_pieces + split_pieces(ref, G)
    starts = doc_starts(cfg, meta)
    items = meta.items
    scale = hd ** (-0.5) * LOG2E
    key_off = token_in_span(cfg, meta, iota((1, cfg.KT), 1))
    row_off = token_in_span(cfg, meta, iota((2 * QH, 1), 0) % QH)
    half = iota((QH, 2 * hd), 1) < hd
    for t in range(cfg.NT):
        go = tile_of(cfg, message_pieces(cfg, go_ref), t)
        prod = go.astype(F32) * tile_of(cfg, split_pieces(o_ref, G), t).astype(F32)
        q_scr[t] = pad_queries(cfg, tile_of(cfg, q_in, t), 0)
        go_scr[t] = pad_queries(cfg, go, 1)
        delta_scr[t, :QH] = jnp.sum(jnp.where(half, prod, 0.0), axis=1, keepdims=True)
        delta_scr[t, QH:] = jnp.sum(jnp.where(half, 0.0, prod), axis=1, keepdims=True)
        acc_scr[t] = jnp.zeros((2 * QH, 2 * hd), F32)

    def step(i, carry):
        parts = []
        for u in range(STEP_QUERY):
            qt, s = items[0, i * STEP_QUERY + u], items[1, i * STEP_QUERY + u]
            kv = tile_of(cfg, kv_pieces, s)
            token = row_off + qt * cfg.span
            key_token = key_off + s * cfg.span
            e = jnp.exp2(mm_nt(q_scr[qt], kv) * scale)
            ds = e * (mm_nt(go_scr[qt], kv) - delta_scr[qt])
            ds = jnp.where((key_token <= token) & (key_token >= start_of(starts, token)), ds, 0.0)
            parts.append((qt, mm(ds.astype(BF), kv)))
        for qt, part in parts:
            acc_scr[qt] += part
        return carry

    lax.fori_loop(0, steps_of(items, STEP_QUERY), step, 0)
    for t in range(cfg.NT):
        acc = acc_scr[t]
        out = jnp.where(half, acc[:QH], pltpu.roll(acc[QH:], hd, 1)) * hd ** (-0.5)
        out = out.astype(BF)
        for k in range(G):
            dq_out[k][t * R : (t + 1) * R, :] = out[k * R : (k + 1) * R]


def grad_key_kernel(cfg, meta, *refs):
    G, T, R, hd, lo, QH, NT = cfg.G, cfg.T, cfg.R, cfg.hd, cfg.lo, cfg.QH, cfg.NT
    own = refs[0]
    q_refs, go_refs = (refs[1 + i * lo : 1 + (i + 1) * lo] for i in range(2))
    rest = refs[1 + 2 * lo :]
    dkv_out, key_scr, value_scr, delta_scr, gk_scr, gv_scr = rest[:G], *rest[G:]
    q_pieces = [piece for ref in q_refs for piece in split_pieces(ref, G)]
    go_pieces = [piece for ref in go_refs for piece in message_pieces(cfg, ref)]
    starts = doc_starts(cfg, meta)
    items = meta.items
    scale = hd ** (-0.5) * LOG2E
    rows = cfg.groups * NT
    for j in range(lo):
        sums = go_refs[j][G * T : G * T + 2 * rows, :].astype(F32)
        sums = sums[:rows] + sums[rows:]
        for t in range(NT):
            for h in range(cfg.groups):
                at = h * NT + t
                delta_scr[t, h : h + 1, j * QH : (j + 1) * QH] = sums[at : at + 1, :QH]
    query_off = token_in_span(cfg, meta, iota((1, cfg.KT), 1))
    row_off = token_in_span(cfg, meta, iota((2 * QH, 1), 0) % QH)
    first = iota((QH, 2 * hd), 1) < hd
    for t in range(NT):
        kv = tile_of(cfg, split_pieces(own, G), t).astype(F32)
        rolled = pltpu.roll(kv, hd, 1)
        keys = [jnp.where(first, kv, 0.0), jnp.where(first, 0.0, rolled)]
        values = [jnp.where(first, rolled, 0.0), jnp.where(first, 0.0, kv)]
        key_scr[t] = jnp.concatenate(keys, axis=0).astype(BF)
        value_scr[t] = jnp.concatenate(values, axis=0).astype(BF)
        gk_scr[t] = jnp.zeros((2 * QH, 2 * hd), F32)
        gv_scr[t] = jnp.zeros((2 * QH, 2 * hd), F32)

    def step(i, carry):
        parts = []
        for u in range(STEP):
            t, kt = items[0, i * STEP + u], items[1, i * STEP + u]
            queries, grads = tile_of(cfg, q_pieces, t), tile_of(cfg, go_pieces, t)
            key_token = row_off + kt * cfg.span
            token = query_off + t * cfg.span
            e = jnp.exp2(mm_nt(key_scr[kt], queries) * scale)
            e = jnp.where((key_token <= token) & (key_token >= start_of(starts, token)), e, 0.0)
            dp = mm_nt(value_scr[kt], grads)
            delta = delta_scr[t]
            ds = [
                (e[:QH] * (dp[:QH] - delta[0:1])).astype(BF),
                (e[QH:] * (dp[QH:] - delta[1:2])).astype(BF),
            ]
            ds = jnp.concatenate(ds, axis=0)
            parts.append((kt, mm(ds, queries), mm(e.astype(BF), grads)))
        for kt, gk, gv in parts:
            gk_scr[kt] += gk
            gv_scr[kt] += gv
        return carry

    lax.fori_loop(0, steps_of(items, STEP), step, 0)
    for t in range(NT):
        gk, gv = gk_scr[t], gv_scr[t]
        gk = (gk[:QH] + pltpu.roll(gk[QH:], hd, 1)) * hd ** (-0.5)
        gv = pltpu.roll(gv[:QH], hd, 1) + gv[QH:]
        out = jnp.where(first, gk, gv).astype(BF)
        for k in range(G):
            dkv_out[k][t * R : (t + 1) * R, :] = out[k * R : (k + 1) * R]


def place_pieces(cfg, hi, scr, pieces):
    w = pieces[0].shape[1]
    for k in range(cfg.G):
        at = pl.multiple_of((hi ^ k) * w, w)
        scr[:, pl.ds(at, w)] = pieces[k][...]


def out_kernel(cfg, meta, *refs):
    G = cfg.G
    wo, ao, part, attn = refs[G:]
    place_pieces(cfg, meta[0] // cfg.lo, attn, refs[:G])
    rows = attn[...]
    part[:, : cfg.D] = mm(rows, wo[...]).astype(BF)
    part[:, cfg.D :] = mm(rows, ao[...]).astype(BF)


def tiles_of(i, count):
    return [
        pl.ds(pl.multiple_of(i * (count * FFN_TILE) + j * FFN_TILE, FFN_TILE), FFN_TILE)
        for j in range(count)
    ]


def hidden_grad_kernel(cfg, meta, cot_ref, wd, bd, ad, out, turned):
    cot = cot_ref[...]
    side = (adapter_mask(cfg, meta) * mm_nt(cot, bd[...])).astype(BF)
    turned[...] = mm(side, slot_select(cfg, meta)).T.astype(BF)

    def part(i, carry):
        for at in tiles_of(i, FFN_STEP):
            out[:, at] = mm_nt(cot, wd[at, :]) + mm_nt(side, ad[at, :])
        return carry

    lax.fori_loop(0, cfg.F // (FFN_STEP * FFN_TILE), part, 0)


def ffn_kernel(
    cfg, units, meta, x_ref, own, other, bo, gain, wg, wu, wd, bg, bu, ag, au, ad, cot_ref, gh, gst,
    mixed_ref, dfn_ref, part_ref, oside, *refs,
):
    D, F = cfg.D, cfg.F
    chunks, (hidden_scr, gg_scr, gu_scr, grads) = refs[: cfg.lo], refs[cfg.lo :]
    flip = meta[0] % cfg.lo
    mask = adapter_mask(cfg, meta)
    select = slot_select(cfg, meta)
    compact = lambda side: mm(side, select).T.astype(BF)
    total = own[...].astype(F32) + other[...].astype(F32)
    out_side = (mask * total[:, D:]).astype(BF)
    oside[...] = mm(out_side, select).astype(BF)
    mixed = x_ref[...].astype(F32) + total[:, :D] + mm(out_side, bo[...])
    mixed_ref[...] = mixed
    rr = lax.rsqrt(jnp.mean(mixed * mixed, axis=-1, keepdims=True) + norm_eps)
    normed = (mixed * rr * gain[...]).astype(BF)
    side_g = (mask * mm(normed, ag[...])).astype(BF)
    side_u = (mask * mm(normed, au[...])).astype(BF)
    turned = compact(side_g), compact(side_u), gst[...]

    def part(i, carry):
        for at in tiles_of(i, FFN_STEP):
            grad_hidden = gh[:, at]
            gate = mm(normed, wg[:, at]) + mm(side_g, bg[:, at])
            upper = mm(normed, wu[:, at]) + mm(side_u, bu[:, at])
            sigma = 1.0 / (1.0 + jnp.exp(-gate))
            silu = gate * sigma
            hidden_scr[:, at] = (silu * upper).astype(BF)
            gg_scr[:, at] = (grad_hidden * upper * (sigma + silu * (1.0 - sigma))).astype(BF)
            gu_scr[:, at] = (grad_hidden * silu).astype(BF)
        return carry

    lax.fori_loop(0, F // (FFN_STEP * FFN_TILE), part, 0)
    tile = FFN_TILE
    side_g = (mask * mm_nt(gg_scr[...], bg[...])).astype(BF)
    side_u = (mask * mm_nt(gu_scr[...], bu[...])).astype(BF)
    side_sum = mm(hidden_scr[...], ad[...])
    for d in range(0, D, tile):
        at = slice(d, d + tile)
        dfn = mm_nt(gg_scr[...], wg[at, :]) + mm_nt(gu_scr[...], wu[at, :])
        dfn_ref[:, at] = (dfn + mm_nt(side_g, ag[at, :]) + mm_nt(side_u, au[at, :])).astype(BF)
    for d in range(0, D, tile):
        at = slice(d, d + tile)
        part_ref[:, at] = mm(hidden_scr[...], wd[:, at]).astype(BF)
    part_ref[:, D:] = side_sum.astype(BF)
    side_d = (mask * side_sum).astype(BF)
    for i, (side, right) in enumerate(((side_g, normed), (side_u, normed), (side_d, cot_ref[...]))):
        units.store(grads, 0, i, mm(compact(side), right).astype(BF))
    for i, right in enumerate((gg_scr, gu_scr, hidden_scr)):
        units.store(grads, 1, i, mm(turned[i], right[...]).astype(BF))
    units.clear_spare(grads)
    for j, chunk in enumerate(chunks):
        for half in range(2):
            chunk[half] = grads[2 * (j ^ flip) + half]


def ffn_call(cfg, units, meta, *ins):
    T, D, F, AW, S = cfg.T, cfg.D, cfg.F, cfg.AW, cfg.S
    return call(
        functools.partial(ffn_kernel, cfg, units),
        [((T, D), F32), ((T, D), BF), ((T, D + AW), BF), ((T, S), BF)]
        + [((2, units.u, 16, 128), BF)] * cfg.lo,
        [meta, *ins],
        scratch=[pltpu.VMEM((T, F), BF)] * 3 + [pltpu.VMEM((units.n, units.u, 16, 128), BF)],
        us=14,
        name="ffn",
    )


def mixed_grad_kernel(cfg, meta, *refs):
    G, D = cfg.G, cfg.D
    mixed_ref, own, other, cot, gain = refs[:5]
    o_in = refs[5 : 5 + G]
    wo, ao, bo, oside = refs[5 + G : 9 + G]
    rest = refs[9 + G :]
    gm_ref, ograds, go_out, attn, go_scr, gm_scr = rest[0], rest[1], rest[2 : 2 + G], *rest[2 + G :]
    hi = meta[0] // cfg.lo
    mixed = mixed_ref[...]
    w = (own[...].astype(F32) + other[...].astype(F32)) * gain[...]
    rr = lax.rsqrt(jnp.mean(mixed * mixed, axis=-1, keepdims=True) + norm_eps)
    inner = jnp.mean(w * mixed, axis=-1, keepdims=True)
    gm = cot[...].astype(F32) + rr * w - (rr * rr * rr * inner) * mixed
    gm_ref[...] = gm
    gmb = gm.astype(BF)
    gm_scr[...] = gmb
    mask = adapter_mask(cfg, meta)
    select = slot_select(cfg, meta)
    grad_side = (mask * mm_nt(gmb, bo[...])).astype(BF)
    go = (mm_nt(gmb, wo[...]) + mm_nt(grad_side, ao[...])).astype(BF)
    w = cfg.groups * cfg.hd
    for h in range(G):
        go_scr[h] = go[:, h * w : (h + 1) * w]
    for k in range(G):
        go_out[k][...] = go_scr[hi ^ k]
    place_pieces(cfg, hi, attn, o_in)
    ograds[0] = mm(mm(grad_side, select).T.astype(BF), attn[...]).astype(BF)
    half = D // 2
    mine = gm_scr[:, pl.ds(pl.multiple_of(meta[1] * half, half), half)]
    ograds[1] = mm(oside[...].astype(F32).T.astype(BF), mine).astype(BF)


def output_kernel(cfg, meta, mixed, own, other, bd, out_ref):
    D = cfg.D
    total = own[...].astype(F32) + other[...].astype(F32)
    side = (adapter_mask(cfg, meta) * total[:, D:]).astype(BF)
    out_ref[...] = (mixed[...] + total[:, :D] + mm(side, bd[...])).astype(BF)


def head_back(cfg, cos, sin, grad, raw, g):
    hd = cfg.hd
    copies = raw.shape[1] // hd
    per = raw.shape[1] // cos.shape[1]
    un = grad * lanes(cos[...], per) - swap_halves(grad, hd) * lanes(sin[...], per)
    w = un * lanes(g[...], copies)
    rr = lax.rsqrt(block_mean(raw * raw, hd) + norm_eps)
    return rr * w - rr * rr * rr * raw * block_mean(w * raw, hd)


def half_lanes(cfg, meta):
    half = cfg.D // 2
    keep = pl.ds(pl.multiple_of(meta[1] * half, half), half)
    send = pl.ds(pl.multiple_of((1 - meta[1]) * half, half), half)
    return keep, send


def query_back_kernel(cfg, meta, *refs):
    G, S = cfg.G, cfg.S
    normed, raw, sides, cos, sin, gain, w, a, b, part, bgrad, akeep, asend, dq_scr, a_scr = refs[G:]
    place_pieces(cfg, meta[0] // cfg.lo, dq_scr, refs[:G])
    g = head_back(cfg, cos, sin, dq_scr[...].astype(F32), raw[...], gain).astype(BF)
    select = slot_select(cfg, meta)
    grad_side = (adapter_mask(cfg, meta) * mm_nt(g, b[...])).astype(BF)
    part[...] = mm_nt(g, w[...]) + mm_nt(grad_side, a[...])
    a_scr[...] = mm(mm(grad_side, select).T.astype(BF), normed[...])
    bgrad[...] = mm(sides[0].astype(F32).T.astype(BF), g).astype(BF)
    keep, send = half_lanes(cfg, meta)
    akeep[...] = a_scr[:, keep].astype(BF)
    asend[...] = a_scr[:, send].astype(BF)


def key_value_side_kernel(cfg, meta, *refs):
    G, S, hd = cfg.G, cfg.S, cfg.hd
    normed, raw, cos, sin, gain, bk, bv, grads, out_sides, akeep, asend, dkv_scr, a_scr = refs[G:]
    place_pieces(cfg, meta[0] // cfg.lo, dkv_scr, refs[:G])
    mask = adapter_mask(cfg, meta)
    select = slot_select(cfg, meta)
    dkv = dkv_scr[...]
    dk = jnp.concatenate([dkv[:, 2 * h * hd : (2 * h + 1) * hd] for h in range(G)], axis=1)
    dv = jnp.concatenate([dkv[:, (2 * h + 1) * hd : (2 * h + 2) * hd] for h in range(G)], axis=1)
    gk = head_back(cfg, cos, sin, dk.astype(F32), raw[...], gain).astype(BF)
    for i, (g, b) in enumerate(((gk, bk), (dv, bv))):
        grad_side = (mask * mm_nt(g, b[...])).astype(BF)
        grads[i] = g
        out_sides[i] = grad_side
        a_scr[i * S : (i + 1) * S, :] = mm(mm(grad_side, select).T.astype(BF), normed[...])
    keep, send = half_lanes(cfg, meta)
    akeep[...] = a_scr[:, keep].astype(BF)
    asend[...] = a_scr[:, send].astype(BF)


def key_value_back_kernel(cfg, meta, grads, grad_sides, sides, wk, wv, ak, av, qpart, part, bgrad):
    total = qpart[...]
    width = grads.shape[2]
    for i, (w, a) in enumerate(((wk, ak), (wv, av))):
        total = total + mm_nt(grads[i], w[...]) + mm_nt(grad_sides[i], a[...])
        bgrad[:, i * width : (i + 1) * width] = mm(
            sides[i].astype(F32).T.astype(BF), grads[i]
        ).astype(BF)
    part[...] = total.astype(BF)


def input_grad_kernel(cfg, meta, x_ref, gain, gm, own, other, out):
    x = x_ref[...].astype(F32)
    w = (own[...].astype(F32) + other[...].astype(F32)) * gain[...]
    rr = lax.rsqrt(jnp.mean(x * x, axis=-1, keepdims=True) + norm_eps)
    inner = jnp.mean(w * x, axis=-1, keepdims=True)
    out[...] = (gm[...] + rr * w - (rr * rr * rr * inner) * x).astype(BF)


class Units:
    def __init__(self, cfg, n, shared, private):
        self.n = n
        self.high = cfg.S // 16
        self.shared, self.private = shared, private
        self.us, self.up = self.per_chunk(shared), self.per_chunk(private)
        self.u = self.us + self.up

    def per_chunk(self, widths):
        return -(-sum(w // 128 for w in widths) * self.high // self.n)

    def places(self, which):
        widths, per, base = (
            (self.shared, self.us, 0) if which == 0 else (self.private, self.up, self.us)
        )
        at, out = 0, []
        for w in widths:
            spots = []
            for c in range(w // 128):
                for a in range(self.high):
                    spots.append((at // per, base + at % per, a, c))
                    at += 1
            out.append(spots)
        return out

    def spare(self):
        out = []
        for widths, per, base in ((self.shared, self.us, 0), (self.private, self.up, self.us)):
            count = sum(w // 128 for w in widths) * self.high
            out += [(i // per, base + i % per) for i in range(count, per * self.n)]
        return out

    def store(self, out, which, array, values, first=0):
        widths, per, base = (
            (self.shared, self.us, 0) if which == 0 else (self.private, self.up, self.us)
        )
        at = sum(w // 128 for w in widths[:array]) * self.high + first * self.high
        for c in range(values.shape[1] // 128):
            for a in range(self.high):
                unit = at + c * self.high + a
                out[unit // per, base + unit % per] = values[
                    a * 16 : a * 16 + 16, c * 128 : c * 128 + 128
                ]

    def clear_spare(self, out):
        for chunk, off in self.spare():
            out[chunk, off] = jnp.zeros((16, 128), BF)


def pack(units, scr, flip, outs, arrays):
    for i, values in enumerate(arrays):
        which = int(i >= len(units.shared))
        units.store(scr, which, i - which * len(units.shared), values)
    units.clear_spare(scr)
    for j, out in enumerate(outs):
        out[...] = scr[j ^ flip]


def add_halves(keep, got, count):
    total = (keep[...].astype(F32) + got[...].astype(F32)).astype(BF)
    rows = total.shape[0] // count
    return [total[i * rows : (i + 1) * rows] for i in range(count)]


def pack_qkv_kernel(cfg, units, meta, keep_q, got_q, keep, got, ograds, bq, bkv, *outs):
    scr, outs = outs[-1], outs[:-1]
    kw = bkv.shape[1] // 2
    shared = add_halves(keep_q, got_q, 1) + add_halves(keep, got, 2) + [ograds[1]]
    private = [ograds[0], bq[...], bkv[:, :kw], bkv[:, kw:]]
    pack(units, scr, meta[0] % cfg.lo, outs, shared + private)


def split_sum_kernel(cfg, meta, *refs):
    *terms, keep, send = refs
    bit = (meta[0] // cfg.lo) % 2
    for out, half in ((keep, bit), (send, 1 - bit)):
        total = terms[0][half].astype(F32)
        for term in terms[1:]:
            total = total + term[half].astype(F32)
        out[...] = total.astype(BF)


def sum_shared_kernel(meta, mine, got, out, shared):
    total = (mine[...].astype(F32) + got[...].astype(F32)).astype(BF)
    out[...] = total
    shared[...] = total[: shared.shape[0]]


def half_shared_kernel(meta, mine, got, out):
    count = got.shape[0]
    at = pl.ds(meta[1] * (count // 2), count // 2)
    out[: count // 2] = (mine[at].astype(F32) + got[at].astype(F32)).astype(BF)
    out[count // 2 :] = mine[count:]


def unpack(read, spots):
    cols = {}
    for chunk, off, a, c in spots:
        cols.setdefault(c, []).append(read(chunk, off))
    return jnp.concatenate([jnp.concatenate(cols[c], axis=0) for c in sorted(cols)], axis=1)


def expand_kernel(cfg, units, plan, halves, meta, *refs):
    own_in, other_in, outs = refs[: cfg.lo], refs[cfg.lo], refs[cfg.lo + 1 : -2]
    own, shared = refs[-2:]
    flip = meta[0] % cfg.lo
    wa = meta[1]
    count = shared.shape[2]
    for j in range(cfg.lo):
        if halves:
            own[j ^ flip] = own_in[j][...]
            shared[wa, j ^ flip] = own_in[j][:count]
            shared[1 - wa, j ^ flip] = other_in[j]
            continue
        for r in range(2):
            at = 2 * (j ^ flip) + (r ^ ((meta[0] // cfg.lo) % 2))
            own[at] = own_in[j][r]
            shared[wa, at] = own_in[j][r, :count]
            shared[1 - wa, at] = other_in[j, r]
    select = slot_select(cfg, meta)

    def write(out, values, transposed, at):
        full = mm(select, values)
        if transposed:
            out[at : at + full.shape[1], :] = full.T
        else:
            out[:, at : at + full.shape[1]] = full

    for (which, i, transposed), out in zip(plan, outs):
        spots = units.places(which)[i]
        if which == 1:
            shift = 0 if halves else count
            write(out, unpack(lambda chunk, off: own[chunk, off - shift], spots), transposed, 0)
        elif halves:
            for w in range(2):
                values = unpack(lambda chunk, off: shared[w, chunk, off], spots)
                write(out, values, transposed, w * values.shape[1])
        else:
            values = unpack(lambda chunk, off: shared[off // count, chunk, off % count], spots)
            write(out, values, transposed, 0)


def upper_bits(cfg):
    bits, bit = [], cfg.n // 2
    while bit >= cfg.lo:
        bits.append(bit)
        bit //= 2
    return bits


def after(*values):
    return lax.optimization_barrier(values)


def swap_cores(value):
    return lax.ppermute(value, "wa", [(0, 1), (1, 0)])


def permute(cfg, value, bits):
    return lax.ppermute(value, "ctx", [(i, i ^ bits) for i in range(cfg.n)])


def per_device(
    hidden_in, attn_gain, query_weight, key_weight, value_weight, query_gain, key_gain, out_weight,
    ffn_gain, gate_weight, up_weight, down_weight, query_adapt_in, query_adapt_out, key_adapt_in,
    key_adapt_out, value_adapt_in, value_adapt_out, out_adapt_in, out_adapt_out, gate_adapt_in,
    gate_adapt_out, up_adapt_in, up_adapt_out, down_adapt_in, down_adapt_out, document_extra,
    document_adapter, cotangent,
):
    head_dim = query_gain.shape[0]
    cfg = Cfg(
        tokens=hidden_in.shape[0],
        n_ctx=lax.axis_size("ctx"),
        heads_kv=key_weight.shape[1] // head_dim,
        groups=query_weight.shape[1] // key_weight.shape[1],
        head_dim=head_dim,
        docs=document_extra.shape[0],
        adapt_width=query_adapt_in.shape[1],
        width=hidden_in.shape[2],
        hidden=gate_weight.shape[1],
    )
    T, D, G, S, AW, n, lo = cfg.T, cfg.D, cfg.G, cfg.S, cfg.AW, cfg.n, cfg.lo
    gw = cfg.groups * head_dim
    QW, KW = query_weight.shape[1], key_weight.shape[1]
    meta = (document_extra, document_adapter)
    x = hidden_in.reshape(T, D)
    cot = cotangent.reshape(T, D)
    gain_a = attn_gain.reshape(1, D)
    gain_f = ffn_gain.reshape(1, D)
    qg = query_gain.reshape(1, head_dim)
    kg = key_gain.reshape(1, head_dim)

    lane = np.arange(2 * head_dim) % (head_dim // 2)
    inverse = np.exp(lane * (-2.0 * math.log(theta_base) / head_dim)).astype(np.float32)[None, :]

    piece = ((T, gw), BF)
    fetched = [
        x, key_adapt_in, value_adapt_in, key_weight, key_adapt_out, value_weight, value_adapt_out,
    ]
    first = call(
        functools.partial(key_value_kernel, cfg),
        [piece] * G
        + [((T, KW), F32), ((2, T, S), BF), ((T, D), BF)]
        + [((T, 2 * head_dim), F32)] * 2,
        [meta, *fetched, gain_a, kg, inverse],
        scratch=[pltpu.VMEM(value.shape, value.dtype) for value in fetched]
        + [pltpu.SemaphoreType.DMA((len(fetched),)), pltpu.VMEM((G, T, 2 * head_dim), BF)],
        us=4,
        name="key_value",
        in_place=len(fetched),
        large=True,
    )
    kv_send = first[:G]
    kraw, sides, normed, cos, sin = first[G:]

    def to_heads(pieces):
        return [pieces[0]] + [permute(cfg, pieces[k], k * lo) for k in range(1, G)]

    def add(values):
        return sum(value.astype(F32) for value in values).astype(BF)

    def to_plane(value):
        return [value] + [permute(cfg, value, j) for j in range(1, lo)]

    kv_heads = to_heads(kv_send)
    second = call(
        functools.partial(query_kernel, cfg),
        [piece] * G + [((T, QW), F32), ((1, T, S), BF), items_shape(cfg)],
        [meta, normed, cos, sin, query_weight, query_adapt_in, query_adapt_out, qg],
        scratch=[pltpu.VMEM((G, T, gw), BF)],
        us=3,
        name="query",
        lists=1,
    )
    q_send, (qraw, side_q, items) = second[:G], second[G:]
    listed = (*meta, items)
    both = list(after(*kv_heads, *q_send))
    kv_heads, q_send = both[:G], both[G:]
    kv = to_plane(jnp.stack(kv_heads))
    q = to_heads(q_send)
    grad_hidden, gst = call(
        functools.partial(hidden_grad_kernel, cfg),
        [((T, cfg.F), F32), ((S, T), BF)],
        [meta, cot, down_weight, down_adapt_out, down_adapt_in],
        us=3,
        name="hidden_grad",
    )
    grad_hidden, *both = after(grad_hidden, *kv, *q)
    kv, q = both[:lo], both[lo:]
    tiles = lambda dtype, width=gw: pltpu.VMEM((cfg.NT, 2 * cfg.QH, width), dtype)
    attn = call(
        functools.partial(attend_kernel, cfg),
        [piece] * G + [((G, T, gw), BF), ((G, T, gw), F32)],
        [listed] + q + kv,
        scratch=[tiles(BF), tiles(F32)],
        us=12,
        name="attend",
    )
    o_send, o_all, linv = attn[:G], attn[G], attn[G + 1]
    o = to_heads(o_send)
    q_stack, _ = after(jnp.stack(q), o_send[0])
    q_plane = to_plane(q_stack)
    (opart,) = call(
        functools.partial(out_kernel, cfg),
        [((T, D + AW), BF)],
        [meta] + o + [out_weight, out_adapt_in],
        scratch=[pltpu.VMEM((T, QW), BF)],
        us=3,
        name="out_proj",
    )
    units_f = Units(cfg, 2 * lo, [D] * 3, [cfg.F] * 3)
    ffn = ffn_call(
        cfg, units_f, meta, x, opart, swap_cores(opart), out_adapt_out, gain_f, gate_weight, up_weight,
        down_weight, gate_adapt_out, up_adapt_out, gate_adapt_in, up_adapt_in, down_adapt_in,
        cot, grad_hidden, gst,
    )
    mixed, dfn, dpart, oside, *parts_f = ffn
    dfn, *q_plane = after(dfn, *q_plane)
    mg = call(
        functools.partial(mixed_grad_kernel, cfg),
        [((T, D), F32), ((2, S, D // 2), BF)] + [piece] * G,
        [meta, mixed, dfn, swap_cores(dfn), cot, gain_f]
        + o
        + [out_weight, out_adapt_in, out_adapt_out, oside],
        scratch=[pltpu.VMEM((T, QW), BF), pltpu.VMEM((G, T, gw), BF), pltpu.VMEM((T, D), BF)],
        us=0.01,
        name="mixed_grad",
    )
    grad_mixed, ograds, go_send = mg[0], mg[1], mg[2:]
    go_heads = to_heads(go_send)
    parts_f = [parts_f[0]] + [permute(cfg, parts_f[j], j) for j in range(1, lo)]
    message = G * T + -(-2 * cfg.groups * cfg.NT // 16) * 16
    (go_all,) = call(
        functools.partial(scale_kernel, cfg),
        [((message, gw), BF)],
        [meta] + go_heads + [linv, o_all],
        scratch=[
            pltpu.VMEM((cfg.NT, cfg.QH, gw), F32),
            pltpu.VMEM((cfg.groups * cfg.NT, gw), F32),
        ],
        us=0.01,
        name="scale",
    )
    go_all, *parts_f = after(go_all, *parts_f)
    sum_f, send_f = call(
        functools.partial(split_sum_kernel, cfg),
        [((units_f.u, 16, 128), BF)] * 2,
        [meta, *parts_f],
        us=0.01,
        name="split_sum",
    )
    go_plane = to_plane(go_all)
    dq_send = call(
        functools.partial(grad_query_kernel, cfg),
        [piece] * G,
        [listed] + q + kv + [go_all, o_all],
        scratch=[tiles(BF), tiles(BF), tiles(F32, 1), tiles(F32)],
        us=13.5,
        name="grad_query",
    )
    near, far = upper_bits(cfg)[1], upper_bits(cfg)[0]
    got_f, *dq_send = after(permute(cfg, send_f, near), *dq_send)
    sum_f = add([sum_f, got_f])
    dq = to_heads(dq_send)
    dkv_send = call(
        functools.partial(grad_key_kernel, cfg),
        [piece] * G,
        [listed, kv[0]] + q_plane + go_plane,
        scratch=[tiles(BF), tiles(BF), pltpu.VMEM((cfg.NT, 16, cfg.KT), F32), tiles(F32)]
        + [tiles(F32)],
        us=16,
        name="grad_key",
    )
    both = list(after(*dq, *dkv_send))
    dq, dkv_send = both[:G], both[G:]
    dkv = to_heads(dkv_send)
    qpart, bgrad_q, akeep_q, asend_q = call(
        functools.partial(query_back_kernel, cfg),
        [((T, D), F32), ((S, QW), BF), ((S, D // 2), BF), ((S, D // 2), BF)],
        [meta]
        + dq
        + [
            normed, qraw, side_q, cos, sin, qg, query_weight, query_adapt_in, query_adapt_out,
        ],
        scratch=[pltpu.VMEM((T, QW), BF), pltpu.VMEM((S, D), F32)],
        us=0.01,
        name="query_back",
    )
    got_f, qpart = after(permute(cfg, sum_f, far), qpart)
    sum_f, shared_f = call(
        sum_shared_kernel,
        [((units_f.u, 16, 128), BF), ((units_f.us, 16, 128), BF)],
        [meta, sum_f, got_f],
        us=0.01,
        name="sum_shared",
    )
    shared_f, qpart, *dkv = after(shared_f, qpart, *dkv)
    kv_grads, kv_sides, akeep_kv, asend_kv = call(
        functools.partial(key_value_side_kernel, cfg),
        [((2, T, KW), BF), ((2, T, AW), BF), ((2 * S, D // 2), BF), ((2 * S, D // 2), BF)],
        [meta] + dkv + [normed, kraw, cos, sin, kg, key_adapt_out, value_adapt_out],
        scratch=[pltpu.VMEM((T, 2 * KW), BF), pltpu.VMEM((2 * S, D), F32)],
        us=0.01,
        name="key_value_side",
    )
    dnormed, bgrad_kv = call(
        functools.partial(key_value_back_kernel, cfg),
        [((T, D), BF), ((S, 2 * KW), BF)],
        [meta, kv_grads, kv_sides, sides, key_weight, value_weight, key_adapt_in, value_adapt_in]
        + [qpart],
        us=0.01,
        name="key_value_back",
    )

    def expand(units, chunks, plan, halves, outs, name):
        shared = units.us if halves else units.us // 2
        theirs = swap_cores(jnp.stack([chunk[..., :shared, :, :] for chunk in chunks]))
        per = chunks[0].shape[-3]
        return call(
            functools.partial(expand_kernel, cfg, units, plan, halves),
            outs,
            [meta, *chunks, theirs],
            scratch=[
                pltpu.VMEM((units.n, per, 16, 128), BF),
                pltpu.VMEM((2, units.n, shared, 16, 128), BF),
            ],
            us=4,
            name=name,
        )

    units_q = Units(cfg, lo, [D // 2] * 4, [QW, QW, KW, KW])
    parts_q = call(
        functools.partial(pack_qkv_kernel, cfg, units_q),
        [((units_q.u, 16, 128), BF)] * lo,
        [meta, akeep_q, swap_cores(asend_q), akeep_kv, swap_cores(asend_kv), ograds, bgrad_q]
        + [bgrad_kv],
        scratch=[pltpu.VMEM((lo, units_q.u, 16, 128), BF)],
        us=0.01,
        name="pack_qkv",
    )
    (sum_f,) = call(
        half_shared_kernel,
        [((units_f.u - units_f.us // 2, 16, 128), BF)],
        [meta, sum_f, swap_cores(shared_f)],
        us=0.01,
        name="half_shared",
    )
    sum_f, dnormed, *parts_q = after(sum_f, dnormed, *parts_q)
    dn_other = swap_cores(dnormed)
    near_f = permute(cfg, sum_f, near)
    sum_q = add([parts_q[0]] + [permute(cfg, parts_q[j], j) for j in range(1, lo)])
    sum_q, dn_other, sum_f, near_f = after(sum_q, dn_other, sum_f, near_f)
    all_f = to_plane(jnp.stack([sum_f, near_f]))
    (input_rows,) = call(
        functools.partial(input_grad_kernel, cfg),
        [((T, D), BF)],
        [meta, x, gain_a, grad_mixed, dnormed, dn_other],
        us=0.01,
        name="input_grad",
    )
    got_q, input_rows = after(permute(cfg, sum_q, near), input_rows)
    sum_q = add([sum_q, got_q])
    got_q, *all_f = after(permute(cfg, sum_q, far), *all_f)
    sum_q, dpart = after(add([sum_q, got_q]), dpart)
    pieces_q = to_plane(sum_q)
    (out_rows,) = call(
        functools.partial(output_kernel, cfg),
        [((T, D), BF)],
        [meta, mixed, dpart, swap_cores(dpart), down_adapt_out],
        us=0.01,
        name="output",
    )
    gate_in, up_in, down_out, gate_out, up_out, down_in = expand(
        units_f,
        all_f,
        [(0, 0, True), (0, 1, True), (0, 2, False), (1, 0, False), (1, 1, False), (1, 2, True)],
        False,
        [((D, AW), F32), ((D, AW), F32), ((AW, D), F32)]
        + [((AW, cfg.F), F32), ((AW, cfg.F), F32), ((cfg.F, AW), F32)],
        "expand_ffn",
    )
    down_out, out_rows, *pieces_q = after(down_out, out_rows, *pieces_q)
    query_in, key_in, value_in, out_out, out_in, query_out, key_out, value_out = expand(
        units_q,
        pieces_q,
        [(0, 0, True), (0, 1, True), (0, 2, True), (0, 3, False)]
        + [(1, 0, True), (1, 1, False), (1, 2, False), (1, 3, False)],
        True,
        [((D, AW), F32)] * 3
        + [((AW, D), F32), ((QW, AW), F32), ((AW, QW), F32), ((AW, KW), F32), ((AW, KW), F32)],
        "expand_qkv",
    )
    return (
        out_rows.reshape(T, 1, D),
        input_rows.reshape(T, 1, D),
        query_in,
        query_out,
        key_in,
        key_out,
        value_in,
        value_out,
        out_in,
        out_out,
        gate_in,
        gate_out,
        up_in,
        up_out,
        down_in,
        down_out,
    )


def solution(mesh):
    return jax.shard_map(
        per_device,
        mesh=mesh,
        in_specs=(
            P(None, "ctx", None), P(), P(None, "wa"), P(None, "wa"), P(None, "wa"), P(), P(),
            P("wa", None), P(), P(None, "wa"), P(None, "wa"), P("wa", None), P(), P(None, "wa"),
            P(), P(None, "wa"), P(), P(None, "wa"), P("wa", None), P(), P(), P(None, "wa"), P(),
            P(None, "wa"), P("wa", None), P(), P(), P(), P(None, "ctx", None),
        ),
        out_specs=(
            P(None, "ctx", None), P(None, "ctx", None), P(), P(None, "wa"), P(), P(None, "wa"), P(),
            P(None, "wa"), P("wa", None), P(), P(), P(None, "wa"), P(), P(None, "wa"),
            P("wa", None), P(),
        ),
        check_vma=False,
    )
```

profile of v0, /device:TPU:0, one launch (start us, length us, event | category | flops | bytes accessed | tf_op | source)
XLA Modules:
  0.0 165.8 jit_solution(8162200482773879524)
XLA Ops:
  0.7 4.6 %key_value.1 = (bf16[256,128]{1,0:T(8,128)(2,1)}, bf16[256,128]{1,0:T(8,128)(2,1)}, bf16[256,128]{1,0:T(8,128)(2,1)}, bf16[256,128]{1,0:T(8,128)(2,1)}, f32[256,...) custom-call(s32[4]{0:T(128)} %refs_0_.41, ...), custom_call_target="tpu_custom_call" | custom-call | flops 4600000000 | tf_op jit(solution)/shard_map/key_value/pallas_call | solution.py:161
  5.3 3.1 %collective-permute-start = (bf16[256,128]{1,0:T(8,128)(2,1)}, bf16[256,128]{1,0:T(8,128)(2,1)S(1)}, u32[]{:S(2)}, u32[]{:S(2)}) collective-permute-start(bf16[256,128]{1,0:T(8,128)(2,1)} %get-tuple-element.174), channel_id=1, source_target_pairs={{0,8},{2,10},{4,12},{6,14},{8,0},{10,2},{12,4},{14,6},{16,24},{18,... | collective-permute-start | bytes 196616 | tf_op jit(solution)/shard_map/ppermute | solution.py:880
  8.4 2.6 %collective-permute-start.1 = (bf16[256,128]{1,0:T(8,128)(2,1)}, bf16[256,128]{1,0:T(8,128)(2,1)S(1)}, u32[]{:S(2)}, u32[]{:S(2)}) collective-permute-start(bf16[256,128]{1,0:T(8,128)(2,1)} %get-tuple-element.175), channel_id=1, source_target_pairs={{0,16},{2,18},{4,20},{6,22},{8,24},{10,26},{12,28},{14,30},{16,0},... | collective-permute-start | bytes 196616 | tf_op jit(solution)/shard_map/ppermute | solution.py:880
  13.9 2.6 %query.1 = (bf16[256,128]{1,0:T(8,128)(2,1)S(1)}, bf16[256,128]{1,0:T(8,128)(2,1)S(1)}, bf16[256,128]{1,0:T(8,128)(2,1)S(1)}, bf16[256,128]{1,0:T(8,128)(2,1)S(1...) custom-call(s32[4]{0:T(128)S(1)} %copy-done.23, s32[4]{0:T(128)S(1)} %copy-done.24, ...), custom_call_target="tpu_custom_call" | custom-call | flops 3449999872 | tf_op jit(solution)/shard_map/query/pallas_call | solution.py:161
  21.1 3.5 %collective-permute-start.7 = (bf16[256,128]{1,0:T(8,128)(2,1)S(1)}, bf16[256,128]{1,0:T(8,128)(2,1)S(1)}, u32[]{:S(2)}, u32[]{:S(2)}) collective-permute-start(bf16[256,128]{1,0:T(8,128)(2,1)S(1)} %get-tuple-element.187), channel_id=1, source_target_pairs={{0,16},{2,18},{4,20},{6,22},{8,24},{10,26},{12,28},{14,30},{16,0},... | collective-permute-start | bytes 196616 | tf_op jit(solution)/shard_map/ppermute | solution.py:880
  25.3 3.1 %hidden_grad.1 = (f32[256,2304]{1,0:T(8,128)S(1)}, bf16[64,256]{1,0:T(8,128)(2,1)S(1)}) custom-call(s32[4]{0:T(128)S(1)} %copy-done.23, s32[4]{0:T(128)S(1)} %copy-done.24, bf16[256,1024]{1,0:T(8,128)(2,1)S(1)} %bitcast.38, bf16[2304,1024]{1,0:T(8,128)(2,1)S(1)} %copy-done.29, bf16[128,1024]{1,0:T(8,128)(2,1)S(1)} %copy-done.17, bf16[2304,128]{1,0:T(8,128)(2,1)S(1)} %copy-done.32), custom_call_target="tpu_custom_call" | custom-call | flops 3449999872 | tf_op jit(solution)/shard_map/hidden_grad/pallas_call | solution.py:161
  28.5 2.2 %collective-permute-done.8.refs_6_ = bf16[256,128]{1,0:T(8,128)(2,1)S(1)} collective-permute-done((bf16[256,128]{1,0:T(8,128)(2,1)S(1)}, bf16[256,128]{1,0:T(8,128)(2,1)S(1)}, u32[]{:S(2)}, u32[]{:S(2)}) %collective-permute-start.8) | collective-permute-done | bytes 65568 | tf_op jit(solution)/shard_map/ppermute | solution.py:880
  31.4 7.0 %attend.1 = (bf16[256,128]{1,0:T(8,128)(2,1)S(1)}, bf16[256,128]{1,0:T(8,128)(2,1)S(1)}, bf16[256,128]{1,0:T(8,128)(2,1)S(1)}, bf16[256,128]{1,0:T(8,128)(2,1)S(...) custom-call(s32[4]{0:T(128)S(1)} %copy-done.23, s32[4]{0:T(128)S(1)} %copy-done.24, ...), custom_call_target="tpu_custom_call" | custom-call | flops 13799999488 | tf_op jit(solution)/shard_map/attend/pallas_call | solution.py:161
  39.9 2.4 %collective-permute-start.10 = (bf16[256,128]{1,0:T(8,128)(2,1)S(1)}, bf16[256,128]{1,0:T(8,128)(2,1)S(1)}, u32[]{:S(2)}, u32[]{:S(2)}) collective-permute-start(bf16[256,128]{1,0:T(8,128)(2,1)S(1)} %get-tuple-element.199), channel_id=1, source_target_pairs={{0,16},{2,18},{4,20},{6,22},{8,24},{10,26},{12,28},{14,30},{16,0},... | collective-permute-start | bytes 196616 | tf_op jit(solution)/shard_map/ppermute | solution.py:880
  43.4 1.9 %collective-permute-done.10.refs_4_.refs_9_ = bf16[256,128]{1,0:T(8,128)(2,1)S(1)} collective-permute-done((bf16[256,128]{1,0:T(8,128)(2,1)S(1)}, bf16[256,128]{1,0:T(8,128)(2,1)S(1)}, u32[]{:S(2)}, u32[]{:S(2)}) %collective-permute-start.10) | collective-permute-done | bytes 65568 | tf_op jit(solution)/shard_map/ppermute | solution.py:880
  45.3 3.1 %collective-permute-done.11.refs_5_.refs_10_ = bf16[256,128]{1,0:T(8,128)(2,1)S(1)} collective-permute-done((bf16[256,128]{1,0:T(8,128)(2,1)S(1)}, bf16[256,128]{1,0:T(8,128)(2,1)S(1)}, u32[]{:S(2)}, u32[]{:S(2)}) %collective-permute-start.11) | collective-permute-done | bytes 65568 | tf_op jit(solution)/shard_map/ppermute | solution.py:880
  53.3 12.0 %ffn.1 = (f32[256,1024]{1,0:T(8,128)S(1)}, bf16[256,1024]{1,0:T(8,128)(2,1)S(1)}, bf16[256,1152]{1,0:T(8,128)(2,1)S(1)}, bf16[256,64]{1,0:T(8,128)(2,1)S(1)}, bf...) custom-call(s32[4]{0:T(128)S(1)} %copy-done.23, ...), custom_call_target="tpu_custom_call" | custom-call | flops 16099999744 | tf_op jit(solution)/shard_map/ffn/pallas_call | solution.py:161
  69.0 2.0 %mixed_grad.1 = (f32[256,1024]{1,0:T(8,128)S(1)}, bf16[2,64,512]{2,1,0:T(8,128)(2,1)S(1)}, bf16[256,128]{1,0:T(8,128)(2,1)S(1)}, bf16[256,128]{1,0:T(8,128)(2,1)...) custom-call(s32[4]{0:T(128)S(1)} %copy-done.23, s32[4]{0:T(128)S(1)} %copy-done.24, ...), custom_call_target="tpu_custom_call" | custom-call | flops 11500000 | tf_op jit(solution)/shard_map/mixed_grad/pallas_call | solution.py:161
  71.1 1.9 %collective-permute-start.18 = (bf16[256,128]{1,0:T(8,128)(2,1)S(1)}, bf16[256,128]{1,0:T(8,128)(2,1)S(1)}, u32[]{:S(2)}, u32[]{:S(2)}) collective-permute-start(bf16[256,128]{1,0:T(8,128)(2,1)S(1)} %get-tuple-element.210), channel_id=1, source_target_pairs={{0,16},{2,18},{4,20},{6,22},{8,24},{10,26},{12,28},{14,30},{16,0},... | collective-permute-start | bytes 196616 | tf_op jit(solution)/shard_map/ppermute | solution.py:880
  73.0 2.7 %collective-permute-done.17.refs_3_ = bf16[256,128]{1,0:T(8,128)(2,1)S(1)} collective-permute-done((bf16[256,128]{1,0:T(8,128)(2,1)S(1)}, bf16[256,128]{1,0:T(8,128)(2,1)S(1)}, u32[]{:S(2)}, u32[]{:S(2)}) %collective-permute-start.17) | collective-permute-done | bytes 65568 | tf_op jit(solution)/shard_map/ppermute | solution.py:880
  78.0 3.8 %collective-permute-done.19.refs_5_ = bf16[256,128]{1,0:T(8,128)(2,1)S(1)} collective-permute-done((bf16[256,128]{1,0:T(8,128)(2,1)S(1)}, bf16[256,128]{1,0:T(8,128)(2,1)S(1)}, u32[]{:S(2)}, u32[]{:S(2)}) %collective-permute-start.19) | collective-permute-done | bytes 65568 | tf_op jit(solution)/shard_map/ppermute | solution.py:880
  87.5 9.2 %grad_query.1 = (bf16[256,128]{1,0:T(8,128)(2,1)S(1)}, bf16[256,128]{1,0:T(8,128)(2,1)S(1)}, bf16[256,128]{1,0:T(8,128)(2,1)S(1)}, bf16[256,128]{1,0:T(8,128)(2,1)S(1)}) custom-call(s32[4]{0:T(128)S(1)} %copy-done.23, s32[4]{0:T(128)S(1)} %copy-done.24, s32[2,47]{1,0:T(2,128)S(1)} %get-tuple-element.171.refs_2_, ...), custom_call_target="tpu_custom_call" | custom-call | flops 15525000192 | tf_op jit(solution)/shard_map/grad_query/pallas_call | solution.py:161
  96.8 2.0 %collective-permute-start.24 = (bf16[39,16,128]{2,1,0:T(8,128)(2,1)S(1)}, bf16[39,16,128]{2,1,0:T(8,128)(2,1)S(1)}, u32[]{:S(2)}, u32[]{:S(2)}) collective-permute-start(bf16[39,16,128]{2,1,0:T(8,128)(2,1)S(1)} %add_convert_fusion.refs_2_), channel_id=1, source_target_pairs={{0,16},{2,18},{4,20},{6,22},{8,24},{10,26},{12,28},{14,30},{16,0},... | collective-permute-start | bytes 479240 | tf_op jit(solution)/shard_map/ppermute | solution.py:880
  100.1 1.8 %collective-permute-start.26 = (bf16[256,128]{1,0:T(8,128)(2,1)S(1)}, bf16[256,128]{1,0:T(8,128)(2,1)S(1)}, u32[]{:S(2)}, u32[]{:S(2)}) collective-permute-start(bf16[256,128]{1,0:T(8,128)(2,1)S(1)} %get-tuple-element.232), channel_id=1, source_target_pairs={{0,16},{2,18},{4,20},{6,22},{8,24},{10,26},{12,28},{14,30},{16,0},... | collective-permute-start | bytes 196616 | tf_op jit(solution)/shard_map/ppermute | solution.py:880
  103.2 10.5 %grad_key.1 = (bf16[256,128]{1,0:T(8,128)(2,1)S(1)}, bf16[256,128]{1,0:T(8,128)(2,1)S(1)}, bf16[256,128]{1,0:T(8,128)(2,1)S(1)}, bf16[256,128]{1,0:T(8,128)(2,1)S(1)}) custom-call(s32[4]{0:T(128)S(1)} %copy-done.23, s32[4]{0:T(128)S(1)} %copy-done.24, s32[2,47]{1,0:T(2,128)S(1)} %get-tuple-element.171.refs_2_, ...), custom_call_target="tpu_custom_call" | custom-call | flops 18400000000 | tf_op jit(solution)/shard_map/grad_key/pallas_call | solution.py:161
  114.2 2.7 %collective-permute-start.32 = (bf16[256,128]{1,0:T(8,128)(2,1)S(1)}, bf16[256,128]{1,0:T(8,128)(2,1)S(1)}, u32[]{:S(2)}, u32[]{:S(2)}) collective-permute-start(bf16[256,128]{1,0:T(8,128)(2,1)S(1)} %get-tuple-element.255), channel_id=1, source_target_pairs={{0,16},{2,18},{4,20},{6,22},{8,24},{10,26},{12,28},{14,30},{16,0},... | collective-permute-start | bytes 196616 | tf_op jit(solution)/shard_map/ppermute | solution.py:880
  118.4 2.1 %query_back.1 = (f32[256,1024]{1,0:T(8,128)S(1)}, bf16[64,512]{1,0:T(8,128)(2,1)S(1)}, bf16[64,512]{1,0:T(8,128)(2,1)S(1)}, bf16[64,512]{1,0:T(8,128)(2,1)S(1)}) custom-call(s32[4]{0:T(128)S(1)} %copy-done.23, s32[4]{0:T(128)S(1)} %copy-done.24, bf16[256,128]{1,0:T(8,128)(2,1)S(1)} %get-tuple-element.242.refs_2_, ...), custom_call_target="tpu_custom_call" | custom-call | flops 11500000 | tf_op jit(solution)/shard_map/query_back/pallas_call | solution.py:161
  121.1 1.8 %collective-permute-done.33.refs_5_ = bf16[256,128]{1,0:T(8,128)(2,1)S(1)} collective-permute-done((bf16[256,128]{1,0:T(8,128)(2,1)S(1)}, bf16[256,128]{1,0:T(8,128)(2,1)S(1)}, u32[]{:S(2)}, u32[]{:S(2)}) %collective-permute-start.33) | collective-permute-done | bytes 65568 | tf_op jit(solution)/shard_map/ppermute | solution.py:880
  123.0 2.0 %key_value_side.1 = (bf16[2,256,256]{2,1,0:T(8,128)(2,1)S(1)}, bf16[2,256,128]{2,1,0:T(8,128)(2,1)S(1)}, bf16[128,512]{1,0:T(8,128)(2,1)S(1)}, bf16[128,512]{1,0:T(8,128)(2,1)S(1)}) custom-call(s32[4]{0:T(128)S(1)} %copy-done.23, s32[4]{0:T(128)S(1)} %copy-done.24, bf16[256,128]{1,0:T(8,128)(2,1)S(1)} %get-tuple-element.258.refs_2_, ...), custom_call_target="tpu_custom_call" | custom-call | flops 11500000 | tf_op jit(solution)/shard_map/key_value_side/pallas_call | solution.py:161
  128.8 1.7 %collective-permute-start.39 = (bf16[28,16,128]{2,1,0:T(8,128)(2,1)S(1)}, bf16[28,16,128]{2,1,0:T(8,128)(2,1)S(1)}, u32[]{:S(2)}, u32[]{:S(2)}) collective-permute-start(bf16[28,16,128]{2,1,0:T(8,128)(2,1)S(1)} %get-tuple-element.282), channel_id=1, source_target_pairs={{0,6},{2,4},{4,2},{6,0},{8,14},{10,12},{12,10},{14,8},{16,22},{18,... | collective-permute-start | bytes 344072 | tf_op jit(solution)/shard_map/ppermute | solution.py:880
  132.3 3.3 %collective-permute-done.39 = bf16[28,16,128]{2,1,0:T(8,128)(2,1)S(1)} collective-permute-done((bf16[28,16,128]{2,1,0:T(8,128)(2,1)S(1)}, bf16[28,16,128]{2,1,0:T(8,128)(2,1)S(1)}, u32[]{:S(2)}, u32[]{:S(2)}) %collective-permute-start.39) | collective-permute-done | bytes 114720 | tf_op jit(solution)/shard_map/ppermute | solution.py:880
  135.6 1.7 %collective-permute-done.38 = bf16[28,16,128]{2,1,0:T(8,128)(2,1)S(1)} collective-permute-done((bf16[28,16,128]{2,1,0:T(8,128)(2,1)S(1)}, bf16[28,16,128]{2,1,0:T(8,128)(2,1)S(1)}, u32[]{:S(2)}, u32[]{:S(2)}) %collective-permute-start.38) | collective-permute-done | bytes 114720 | tf_op jit(solution)/shard_map/ppermute | solution.py:880
  141.1 1.9 %input_grad.1 = bf16[256,1024]{1,0:T(8,128)(2,1)} custom-call(s32[4]{0:T(128)S(1)} %copy-done.23, s32[4]{0:T(128)S(1)} %copy-done.24, bf16[256,1024]{1,0:T(8,128)(2,1)S(1)} %bitcast.37, f32[1,1024]{1,0:T(1,128)S(1)} %bitcast.46, f32[256,1024]{1,0:T(8,128)S(1)} %get-tuple-element.286.refs_4_, bf16[256,1024]{1,0:T(8,128)(2,1)S(1)} %get-tuple-element.283.refs_5_, ...), custom_call_target="tpu_custom_call" | custom-call | flops 11500000 | tf_op jit(solution)/shard_map/input_grad/pallas_call | solution.py:161
  143.0 2.0 %collective-permute-start.43 = (bf16[28,16,128]{2,1,0:T(8,128)(2,1)S(1)}, bf16[28,16,128]{2,1,0:T(8,128)(2,1)S(1)}, u32[]{:S(2)}, u32[]{:S(2)}) collective-permute-start(bf16[28,16,128]{2,1,0:T(8,128)(2,1)S(1)} %add_convert_fusion.2), channel_id=1, source_target_pairs={{0,16},{2,18},{4,20},{6,22},{8,24},{10,26},{12,28},{14,30},{16,0},... | collective-permute-start | bytes 344072 | tf_op jit(solution)/shard_map/ppermute | solution.py:880
  145.0 5.7 %collective-permute-done.43 = bf16[28,16,128]{2,1,0:T(8,128)(2,1)S(1)} collective-permute-done((bf16[28,16,128]{2,1,0:T(8,128)(2,1)S(1)}, bf16[28,16,128]{2,1,0:T(8,128)(2,1)S(1)}, u32[]{:S(2)}, u32[]{:S(2)}) %collective-permute-start.43) | collective-permute-done | bytes 114720 | tf_op jit(solution)/shard_map/ppermute | solution.py:880
  156.6 3.3 %expand_ffn.1 = (f32[1024,128]{1,0:T(8,128)}, f32[1024,128]{1,0:T(8,128)}, f32[128,1024]{1,0:T(8,128)}, f32[128,2304]{1,0:T(8,128)}, f32[128,2304]{1,0:T(8,128)}, /*index=5*/f32[2304,128]{1,0:T(8,128)}) custom-call(s32[4]{0:T(128)S(1)} %copy-done.23, s32[4]{0:T(128)S(1)} %copy-done.24, bf16[2,33,16,128]{3,2,1,0:T(8,128)(2,1)S(1)} %pad_maximum_fusion.refs_2_, ...), custom_call_target="tpu_custom_call" | custom-call | flops 4600000000 | tf_op jit(solution)/shard_map/expand_ffn/pallas_call | solution.py:161
  163.3 2.5 %expand_qkv.1 = (f32[1024,128]{1,0:T(8,128)}, f32[1024,128]{1,0:T(8,128)}, f32[1024,128]{1,0:T(8,128)}, f32[128,1024]{1,0:T(8,128)}, f32[512,128]{1,0:T(8,128)},...) custom-call(s32[4]{0:T(128)S(1)} %copy-done.23, s32[4]{0:T(128)S(1)} %copy-done.24, ...), custom_call_target="tpu_custom_call" | custom-call | flops 4600000000 | tf_op jit(solution)/shard_map/expand_qkv/pallas_call | solution.py:161
  (192 shorter events, 51.6 us)
Async XLA Ops:
  5.3 11.2 %collective-permute-start = (bf16[256,128]{1,0:T(8,128)(2,1)}, bf16[256,128]{1,0:T(8,128)(2,1)S(1)}, u32[]{:S(2)}, u32[]{:S(2)}) collective-permute-start(bf16[256,128]{1,0:T(8,128)(2,1)} %get-tuple-element.174), channel_id=1, source_target_pairs={{0,8},{2,10},{4,12},{6,14},{8,0},{10,2},{12,4},{14,6},{16,24},{18,... | collective-permute-start | bytes 196616 | tf_op jit(solution)/shard_map/ppermute | solution.py:880
  8.4 8.2 %collective-permute-start.1 = (bf16[256,128]{1,0:T(8,128)(2,1)}, bf16[256,128]{1,0:T(8,128)(2,1)S(1)}, u32[]{:S(2)}, u32[]{:S(2)}) collective-permute-start(bf16[256,128]{1,0:T(8,128)(2,1)} %get-tuple-element.175), channel_id=1, source_target_pairs={{0,16},{2,18},{4,20},{6,22},{8,24},{10,26},{12,28},{14,30},{16,0},... | collective-permute-start | bytes 196616 | tf_op jit(solution)/shard_map/ppermute | solution.py:880
  17.3 7.3 %collective-permute-start.6 = (bf16[256,128]{1,0:T(8,128)(2,1)S(1)}, bf16[256,128]{1,0:T(8,128)(2,1)S(1)}, u32[]{:S(2)}, u32[]{:S(2)}) collective-permute-start(bf16[256,128]{1,0:T(8,128)(2,1)S(1)} %get-tuple-element.186), channel_id=1, source_target_pairs={{0,8},{2,10},{4,12},{6,14},{8,0},{10,2},{12,4},{14,6},{16,24},{18,... | collective-permute-start | bytes 196616 | tf_op jit(solution)/shard_map/ppermute | solution.py:880
  17.6 13.1 %collective-permute-start.3 = (bf16[4,256,128]{2,1,0:T(8,128)(2,1)S(1)}, bf16[4,256,128]{2,1,0:T(8,128)(2,1)S(1)}, u32[]{:S(2)}, u32[]{:S(2)}) collective-permute-start(bf16[4,256,128]{2,1,0:T(8,128)(2,1)S(1)} %pad_maximum_fusion.1.refs_7_.refs_3_), channel_id=1, source_target_pairs={{0,2},{2,0},{4,6},{6,4},{8,10},{10,8},{12,14},{14,12},{16,18},{18,... | collective-permute-start | bytes 786440 | tf_op jit(solution)/shard_map/ppermute | solution.py:880
  19.1 12.3 %collective-permute-start.4 = (bf16[4,256,128]{2,1,0:T(8,128)(2,1)S(1)}, bf16[4,256,128]{2,1,0:T(8,128)(2,1)S(1)}, u32[]{:S(2)}, u32[]{:S(2)}) collective-permute-start(bf16[4,256,128]{2,1,0:T(8,128)(2,1)S(1)} %pad_maximum_fusion.1.refs_7_.refs_3_), channel_id=1, source_target_pairs={{0,4},{2,6},{4,0},{6,2},{8,12},{10,14},{12,8},{14,10},{16,20},{18,... | collective-permute-start | bytes 786440 | tf_op jit(solution)/shard_map/ppermute | solution.py:880
  20.6 10.7 %collective-permute-start.5 = (bf16[4,256,128]{2,1,0:T(8,128)(2,1)S(1)}, bf16[4,256,128]{2,1,0:T(8,128)(2,1)S(1)}, u32[]{:S(2)}, u32[]{:S(2)}) collective-permute-start(bf16[4,256,128]{2,1,0:T(8,128)(2,1)S(1)} %pad_maximum_fusion.1.refs_7_.refs_3_), channel_id=1, source_target_pairs={{0,6},{2,4},{4,2},{6,0},{8,14},{10,12},{12,10},{14,8},{16,22},{18,... | collective-permute-start | bytes 786440 | tf_op jit(solution)/shard_map/ppermute | solution.py:880
  21.1 7.3 %collective-permute-start.7 = (bf16[256,128]{1,0:T(8,128)(2,1)S(1)}, bf16[256,128]{1,0:T(8,128)(2,1)S(1)}, u32[]{:S(2)}, u32[]{:S(2)}) collective-permute-start(bf16[256,128]{1,0:T(8,128)(2,1)S(1)} %get-tuple-element.187), channel_id=1, source_target_pairs={{0,16},{2,18},{4,20},{6,22},{8,24},{10,26},{12,28},{14,30},{16,0},... | collective-permute-start | bytes 196616 | tf_op jit(solution)/shard_map/ppermute | solution.py:880
  49.7 15.7 %collective-permute-start.13 = (bf16[4,256,128]{2,1,0:T(8,128)(2,1)S(1)}, bf16[4,256,128]{2,1,0:T(8,128)(2,1)S(1)}, u32[]{:S(2)}, u32[]{:S(2)}) collective-permute-start(bf16[4,256,128]{2,1,0:T(8,128)(2,1)S(1)} %pad_maximum_fusion.2.refs_4_), channel_id=1, source_target_pairs={{0,2},{2,0},{4,6},{6,4},{8,10},{10,8},{12,14},{14,12},{16,18},{18,... | collective-permute-start | bytes 786440 | tf_op jit(solution)/shard_map/ppermute | solution.py:880
  50.9 14.4 %collective-permute-start.14 = (bf16[4,256,128]{2,1,0:T(8,128)(2,1)S(1)}, bf16[4,256,128]{2,1,0:T(8,128)(2,1)S(1)}, u32[]{:S(2)}, u32[]{:S(2)}) collective-permute-start(bf16[4,256,128]{2,1,0:T(8,128)(2,1)S(1)} %pad_maximum_fusion.2.refs_4_), channel_id=1, source_target_pairs={{0,4},{2,6},{4,0},{6,2},{8,12},{10,14},{12,8},{14,10},{16,20},{18,... | collective-permute-start | bytes 786440 | tf_op jit(solution)/shard_map/ppermute | solution.py:880
  51.8 13.6 %collective-permute-start.15 = (bf16[4,256,128]{2,1,0:T(8,128)(2,1)S(1)}, bf16[4,256,128]{2,1,0:T(8,128)(2,1)S(1)}, u32[]{:S(2)}, u32[]{:S(2)}) collective-permute-start(bf16[4,256,128]{2,1,0:T(8,128)(2,1)S(1)} %pad_maximum_fusion.2.refs_4_), channel_id=1, source_target_pairs={{0,6},{2,4},{4,2},{6,0},{8,14},{10,12},{12,10},{14,8},{16,22},{18,... | collective-permute-start | bytes 786440 | tf_op jit(solution)/shard_map/ppermute | solution.py:880
  65.5 17.3 %collective-permute-start.20 = (bf16[2,39,16,128]{3,2,1,0:T(8,128)(2,1)S(1)}, bf16[2,39,16,128]{3,2,1,0:T(8,128)(2,1)S(1)}, u32[]{:S(2)}, u32[]{:S(2)}) collective-permute-start(bf16[2,39,16,128]{3,2,1,0:T(8,128)(2,1)S(1)} %get-tuple-element.215), channel_id=1, source_target_pairs={{0,2},{2,0},{4,6},{6,4},{8,10},{10,8},{12,14},{14,12},{16,18},{18,... | collective-permute-start | bytes 958472 | tf_op jit(solution)/shard_map/ppermute | solution.py:880
  66.8 16.0 %collective-permute-start.21 = (bf16[2,39,16,128]{3,2,1,0:T(8,128)(2,1)S(1)}, bf16[2,39,16,128]{3,2,1,0:T(8,128)(2,1)S(1)}, u32[]{:S(2)}, u32[]{:S(2)}) collective-permute-start(bf16[2,39,16,128]{3,2,1,0:T(8,128)(2,1)S(1)} %get-tuple-element.216), channel_id=1, source_target_pairs={{0,4},{2,6},{4,0},{6,2},{8,12},{10,14},{12,8},{14,10},{16,20},{18,... | collective-permute-start | bytes 958472 | tf_op jit(solution)/shard_map/ppermute | solution.py:880
  67.6 15.6 %collective-permute-start.22 = (bf16[2,39,16,128]{3,2,1,0:T(8,128)(2,1)S(1)}, bf16[2,39,16,128]{3,2,1,0:T(8,128)(2,1)S(1)}, u32[]{:S(2)}, u32[]{:S(2)}) collective-permute-start(bf16[2,39,16,128]{3,2,1,0:T(8,128)(2,1)S(1)} %get-tuple-element.217), channel_id=1, source_target_pairs={{0,6},{2,4},{4,2},{6,0},{8,14},{10,12},{12,10},{14,8},{16,22},{18,... | collective-permute-start | bytes 958472 | tf_op jit(solution)/shard_map/ppermute | solution.py:880
  71.1 6.8 %collective-permute-start.18 = (bf16[256,128]{1,0:T(8,128)(2,1)S(1)}, bf16[256,128]{1,0:T(8,128)(2,1)S(1)}, u32[]{:S(2)}, u32[]{:S(2)}) collective-permute-start(bf16[256,128]{1,0:T(8,128)(2,1)S(1)} %get-tuple-element.210), channel_id=1, source_target_pairs={{0,16},{2,18},{4,20},{6,22},{8,24},{10,26},{12,28},{14,30},{16,0},... | collective-permute-start | bytes 196616 | tf_op jit(solution)/shard_map/ppermute | solution.py:880
  83.2 16.8 %collective-permute-start.28 = (bf16[1056,128]{1,0:T(8,128)(2,1)S(1)}, bf16[1056,128]{1,0:T(8,128)(2,1)S(1)}, u32[]{:S(2)}, u32[]{:S(2)}) collective-permute-start(bf16[1056,128]{1,0:T(8,128)(2,1)S(1)} %scale.1.refs_11_.refs_8_), channel_id=1, source_target_pairs={{0,2},{2,0},{4,6},{6,4},{8,10},{10,8},{12,14},{14,12},{16,18},{18,... | collective-permute-start | bytes 811016 | tf_op jit(solution)/shard_map/ppermute | solution.py:880
  84.1 17.8 %collective-permute-start.29 = (bf16[1056,128]{1,0:T(8,128)(2,1)S(1)}, bf16[1056,128]{1,0:T(8,128)(2,1)S(1)}, u32[]{:S(2)}, u32[]{:S(2)}) collective-permute-start(bf16[1056,128]{1,0:T(8,128)(2,1)S(1)} %scale.1.refs_11_.refs_8_), channel_id=1, source_target_pairs={{0,4},{2,6},{4,0},{6,2},{8,12},{10,14},{12,8},{14,10},{16,20},{18,... | collective-permute-start | bytes 811016 | tf_op jit(solution)/shard_map/ppermute | solution.py:880
  85.5 17.7 %collective-permute-start.30 = (bf16[1056,128]{1,0:T(8,128)(2,1)S(1)}, bf16[1056,128]{1,0:T(8,128)(2,1)S(1)}, u32[]{:S(2)}, u32[]{:S(2)}) collective-permute-start(bf16[1056,128]{1,0:T(8,128)(2,1)S(1)} %scale.1.refs_11_.refs_8_), channel_id=1, source_target_pairs={{0,6},{2,4},{4,2},{6,0},{8,14},{10,12},{12,10},{14,8},{16,22},{18,... | collective-permute-start | bytes 811016 | tf_op jit(solution)/shard_map/ppermute | solution.py:880
  87.4 9.3 %collective-permute-start.23 = (bf16[39,16,128]{2,1,0:T(8,128)(2,1)S(1)}, bf16[39,16,128]{2,1,0:T(8,128)(2,1)S(1)}, u32[]{:S(2)}, u32[]{:S(2)}) collective-permute-start(bf16[39,16,128]{2,1,0:T(8,128)(2,1)S(1)} %get-tuple-element.223), channel_id=1, source_target_pairs={{0,8},{2,10},{4,12},{6,14},{8,0},{10,2},{12,4},{14,6},{16,24},{18,... | collective-permute-start | bytes 479240 | tf_op jit(solution)/shard_map/ppermute | solution.py:880
  96.8 23.7 %collective-permute-start.24 = (bf16[39,16,128]{2,1,0:T(8,128)(2,1)S(1)}, bf16[39,16,128]{2,1,0:T(8,128)(2,1)S(1)}, u32[]{:S(2)}, u32[]{:S(2)}) collective-permute-start(bf16[39,16,128]{2,1,0:T(8,128)(2,1)S(1)} %add_convert_fusion.refs_2_), channel_id=1, source_target_pairs={{0,16},{2,18},{4,20},{6,22},{8,24},{10,26},{12,28},{14,30},{16,0},... | collective-permute-start | bytes 479240 | tf_op jit(solution)/shard_map/ppermute | solution.py:880
  98.8 15.0 %collective-permute-start.25 = (bf16[256,128]{1,0:T(8,128)(2,1)S(1)}, bf16[256,128]{1,0:T(8,128)(2,1)S(1)}, u32[]{:S(2)}, u32[]{:S(2)}) collective-permute-start(bf16[256,128]{1,0:T(8,128)(2,1)S(1)} %get-tuple-element.231), channel_id=1, source_target_pairs={{0,8},{2,10},{4,12},{6,14},{8,0},{10,2},{12,4},{14,6},{16,24},{18,... | collective-permute-start | bytes 196616 | tf_op jit(solution)/shard_map/ppermute | solution.py:880
  100.1 13.8 %collective-permute-start.26 = (bf16[256,128]{1,0:T(8,128)(2,1)S(1)}, bf16[256,128]{1,0:T(8,128)(2,1)S(1)}, u32[]{:S(2)}, u32[]{:S(2)}) collective-permute-start(bf16[256,128]{1,0:T(8,128)(2,1)S(1)} %get-tuple-element.232), channel_id=1, source_target_pairs={{0,16},{2,18},{4,20},{6,22},{8,24},{10,26},{12,28},{14,30},{16,0},... | collective-permute-start | bytes 196616 | tf_op jit(solution)/shard_map/ppermute | solution.py:880
  101.8 12.0 %collective-permute-start.27 = (bf16[256,128]{1,0:T(8,128)(2,1)S(1)}, bf16[256,128]{1,0:T(8,128)(2,1)S(1)}, u32[]{:S(2)}, u32[]{:S(2)}) collective-permute-start(bf16[256,128]{1,0:T(8,128)(2,1)S(1)} %get-tuple-element.233), channel_id=1, source_target_pairs={{0,24},{2,26},{4,28},{6,30},{8,16},{10,18},{12,20},{14,22},{16,8},... | collective-permute-start | bytes 196616 | tf_op jit(solution)/shard_map/ppermute | solution.py:880
  113.8 7.3 %collective-permute-start.31 = (bf16[256,128]{1,0:T(8,128)(2,1)S(1)}, bf16[256,128]{1,0:T(8,128)(2,1)S(1)}, u32[]{:S(2)}, u32[]{:S(2)}) collective-permute-start(bf16[256,128]{1,0:T(8,128)(2,1)S(1)} %get-tuple-element.254), channel_id=1, source_target_pairs={{0,8},{2,10},{4,12},{6,14},{8,0},{10,2},{12,4},{14,6},{16,24},{18,... | collective-permute-start | bytes 196616 | tf_op jit(solution)/shard_map/ppermute | solution.py:880
  114.2 6.9 %collective-permute-start.32 = (bf16[256,128]{1,0:T(8,128)(2,1)S(1)}, bf16[256,128]{1,0:T(8,128)(2,1)S(1)}, u32[]{:S(2)}, u32[]{:S(2)}) collective-permute-start(bf16[256,128]{1,0:T(8,128)(2,1)S(1)} %get-tuple-element.255), channel_id=1, source_target_pairs={{0,16},{2,18},{4,20},{6,22},{8,24},{10,26},{12,28},{14,30},{16,0},... | collective-permute-start | bytes 196616 | tf_op jit(solution)/shard_map/ppermute | solution.py:880
  128.3 9.1 %collective-permute-start.40 = (bf16[256,1024]{1,0:T(8,128)(2,1)S(1)}, bf16[256,1024]{1,0:T(8,128)(2,1)S(1)}, u32[]{:S(2)}, u32[]{:S(2)}) collective-permute-start(bf16[256,1024]{1,0:T(8,128)(2,1)S(1)} %get-tuple-element.283.refs_5_), channel_id=1, source_target_pairs={{0,1},{1,0},{2,3},{3,2},{4,5},{5,4},{6,7},{7,6},{8,9},{9,8},{10,11... | collective-permute-start | bytes 1572872 | tf_op jit(solution)/shard_map/ppermute | solution.py:876
  137.5 13.1 %collective-permute-start.44 = (bf16[2,33,16,128]{3,2,1,0:T(8,128)(2,1)S(1)}, bf16[2,33,16,128]{3,2,1,0:T(8,128)(2,1)S(1)}, u32[]{:S(2)}, u32[]{:S(2)}) collective-permute-start(bf16[2,33,16,128]{3,2,1,0:T(8,128)(2,1)S(1)} %pad_maximum_fusion.refs_2_), channel_id=1, source_target_pairs={{0,2},{2,0},{4,6},{6,4},{8,10},{10,8},{12,14},{14,12},{16,18},{18,... | collective-permute-start | bytes 811016 | tf_op jit(solution)/shard_map/ppermute | solution.py:880
  138.5 12.9 %collective-permute-start.45 = (bf16[2,33,16,128]{3,2,1,0:T(8,128)(2,1)S(1)}, bf16[2,33,16,128]{3,2,1,0:T(8,128)(2,1)S(1)}, u32[]{:S(2)}, u32[]{:S(2)}) collective-permute-start(bf16[2,33,16,128]{3,2,1,0:T(8,128)(2,1)S(1)} %pad_maximum_fusion.refs_2_), channel_id=1, source_target_pairs={{0,4},{2,6},{4,0},{6,2},{8,12},{10,14},{12,8},{14,10},{16,20},{18,... | collective-permute-start | bytes 811016 | tf_op jit(solution)/shard_map/ppermute | solution.py:880
  139.9 12.5 %collective-permute-start.46 = (bf16[2,33,16,128]{3,2,1,0:T(8,128)(2,1)S(1)}, bf16[2,33,16,128]{3,2,1,0:T(8,128)(2,1)S(1)}, u32[]{:S(2)}, u32[]{:S(2)}) collective-permute-start(bf16[2,33,16,128]{3,2,1,0:T(8,128)(2,1)S(1)} %pad_maximum_fusion.refs_2_), channel_id=1, source_target_pairs={{0,6},{2,4},{4,2},{6,0},{8,14},{10,12},{12,10},{14,8},{16,22},{18,... | collective-permute-start | bytes 811016 | tf_op jit(solution)/shard_map/ppermute | solution.py:880
  143.0 7.6 %collective-permute-start.43 = (bf16[28,16,128]{2,1,0:T(8,128)(2,1)S(1)}, bf16[28,16,128]{2,1,0:T(8,128)(2,1)S(1)}, u32[]{:S(2)}, u32[]{:S(2)}) collective-permute-start(bf16[28,16,128]{2,1,0:T(8,128)(2,1)S(1)} %add_convert_fusion.2), channel_id=1, source_target_pairs={{0,16},{2,18},{4,20},{6,22},{8,24},{10,26},{12,28},{14,30},{16,0},... | collective-permute-start | bytes 344072 | tf_op jit(solution)/shard_map/ppermute | solution.py:880
  152.6 7.3 %collective-permute-start.48 = (bf16[256,1152]{1,0:T(8,128)(2,1)S(1)}, bf16[256,1152]{1,0:T(8,128)(2,1)S(1)}, u32[]{:S(2)}, u32[]{:S(2)}) collective-permute-start(bf16[256,1152]{1,0:T(8,128)(2,1)S(1)} %get-tuple-element.298.refs_3_), channel_id=1, source_target_pairs={{0,1},{1,0},{2,3},{3,2},{4,5},{5,4},{6,7},{7,6},{8,9},{9,8},{10,11... | collective-permute-start | bytes 1769480 | tf_op jit(solution)/shard_map/ppermute | solution.py:876
  153.1 8.4 %collective-permute-start.49 = (bf16[28,16,128]{2,1,0:T(8,128)(2,1)S(1)}, bf16[28,16,128]{2,1,0:T(8,128)(2,1)S(1)}, u32[]{:S(2)}, u32[]{:S(2)}) collective-permute-start(bf16[28,16,128]{2,1,0:T(8,128)(2,1)S(1)} %add_convert_fusion.1.refs_2_), channel_id=1, source_target_pairs={{0,2},{2,0},{4,6},{6,4},{8,10},{10,8},{12,14},{14,12},{16,18},{18,... | collective-permute-start | bytes 344072 | tf_op jit(solution)/shard_map/ppermute | solution.py:880
  154.3 7.2 %collective-permute-start.50 = (bf16[28,16,128]{2,1,0:T(8,128)(2,1)S(1)}, bf16[28,16,128]{2,1,0:T(8,128)(2,1)S(1)}, u32[]{:S(2)}, u32[]{:S(2)}) collective-permute-start(bf16[28,16,128]{2,1,0:T(8,128)(2,1)S(1)} %add_convert_fusion.1.refs_2_), channel_id=1, source_target_pairs={{0,4},{2,6},{4,0},{6,2},{8,12},{10,14},{12,8},{14,10},{16,20},{18,... | collective-permute-start | bytes 344072 | tf_op jit(solution)/shard_map/ppermute | solution.py:880
  (61 other events, 537.1 us)
where the time goes:
time: 166 us
  Pallas kernels  70.5 us (42%)
  starting transfers between devices  58.2 us (35%)
  waiting for transfers between devices  32.2 us (19%)
  local copies, waits for them, and re-layouts  3.09 us (2%)
    pallas_call x21, Pallas kernels, call(): pl.pallas_call(with_meta(kernel, count), out_shape=[jax.ShapeDtypeStruct(...  70.5 us
    ppermute x44, starting transfers between devices, permute(): return lax.ppermute(value, 'ctx', [(i, i ^ bits) for i in range(cfg.n)])  56.2 us
    ppermute x44, waiting for transfers between devices, permute(): return lax.ppermute(value, 'ctx', [(i, i ^ bits) for i in range(cfg.n)])  30.6 us
  transfers between devices with their start and end apart: 53, of which 17 were waited for; matrix products, arithmetic and copies ran while one was open for 0% of the time, Pallas kernels for 32%

commit v1 on v0

--- a/solution.py
+++ b/solution.py
@@ -539,11 +539,11 @@
 
 
 def ffn_kernel(
-    cfg, units, meta, x_ref, own, other, bo, gain, wg, wu, wd, bg, bu, ag, au, ad, cot_ref, gh, gst,
-    mixed_ref, dfn_ref, part_ref, oside, *refs,
+    cfg, units, meta, x_ref, own, other, bo, gain, wg, wu, bg, bu, ag, au, ad, cot_ref, gh, gst,
+    mixed_ref, dfn_ref, hidden_scr, side_ref, oside, *refs,
 ):
     D, F = cfg.D, cfg.F
-    chunks, (hidden_scr, gg_scr, gu_scr, grads) = refs[: cfg.lo], refs[cfg.lo :]
+    chunks, (gg_scr, gu_scr, grads) = refs[: cfg.lo], refs[cfg.lo :]
     flip = meta[0] % cfg.lo
     mask = adapter_mask(cfg, meta)
     select = slot_select(cfg, meta)
@@ -580,10 +580,7 @@
         at = slice(d, d + tile)
         dfn = mm_nt(gg_scr[...], wg[at, :]) + mm_nt(gu_scr[...], wu[at, :])
         dfn_ref[:, at] = (dfn + mm_nt(side_g, ag[at, :]) + mm_nt(side_u, au[at, :])).astype(BF)
-    for d in range(0, D, tile):
-        at = slice(d, d + tile)
-        part_ref[:, at] = mm(hidden_scr[...], wd[:, at]).astype(BF)
-    part_ref[:, D:] = side_sum.astype(BF)
+    side_ref[...] = side_sum.astype(BF)
     side_d = (mask * side_sum).astype(BF)
     for i, (side, right) in enumerate(((side_g, normed), (side_u, normed), (side_d, cot_ref[...]))):
         units.store(grads, 0, i, mm(compact(side), right).astype(BF))
@@ -599,10 +596,10 @@
     T, D, F, AW, S = cfg.T, cfg.D, cfg.F, cfg.AW, cfg.S
     return call(
         functools.partial(ffn_kernel, cfg, units),
-        [((T, D), F32), ((T, D), BF), ((T, D + AW), BF), ((T, S), BF)]
+        [((T, D), F32), ((T, D), BF), ((T, F), BF), ((T, AW), BF), ((T, S), BF)]
         + [((2, units.u, 16, 128), BF)] * cfg.lo,
         [meta, *ins],
-        scratch=[pltpu.VMEM((T, F), BF)] * 3 + [pltpu.VMEM((units.n, units.u, 16, 128), BF)],
+        scratch=[pltpu.VMEM((T, F), BF)] * 2 + [pltpu.VMEM((units.n, units.u, 16, 128), BF)],
         us=14,
         name="ffn",
     )
@@ -640,6 +637,11 @@
     ograds[1] = mm(oside[...].astype(F32).T.astype(BF), mine).astype(BF)
 
 
+def down_kernel(cfg, meta, hidden, wd, side, part):
+    part[:, : cfg.D] = mm(hidden[...], wd[...]).astype(BF)
+    part[:, cfg.D :] = side[...]
+
+
 def output_kernel(cfg, meta, mixed, own, other, bd, out_ref):
     D = cfg.D
     total = own[...].astype(F32) + other[...].astype(F32)
@@ -681,8 +683,11 @@
 
 def key_value_side_kernel(cfg, meta, *refs):
     G, S, hd = cfg.G, cfg.S, cfg.hd
-    normed, raw, cos, sin, gain, bk, bv, grads, out_sides, akeep, asend, dkv_scr, a_scr = refs[G:]
-    place_pieces(cfg, meta[0] // cfg.lo, dkv_scr, refs[:G])
+    dkv_in = refs[:G]
+    normed, raw, cos, sin, gain, bk, bv, mine, got, *refs = refs[G:]
+    grads, out_sides, akeep, asend, chunk, dkv_scr, a_scr = refs
+    half_shared(meta, mine, got, chunk)
+    place_pieces(cfg, meta[0] // cfg.lo, dkv_scr, dkv_in)
     mask = adapter_mask(cfg, meta)
     select = slot_select(cfg, meta)
     dkv = dkv_scr[...]
@@ -699,7 +704,9 @@
     asend[...] = a_scr[:, send].astype(BF)
 
 
-def key_value_back_kernel(cfg, meta, grads, grad_sides, sides, wk, wv, ak, av, qpart, part, bgrad):
+def key_value_back_kernel(
+    cfg, meta, grads, grad_sides, sides, wk, wv, ak, av, qpart, part, bgrad
+):
     total = qpart[...]
     width = grads.shape[2]
     for i, (w, a) in enumerate(((wk, ak), (wv, av))):
@@ -806,7 +813,7 @@
     shared[...] = total[: shared.shape[0]]
 
 
-def half_shared_kernel(meta, mine, got, out):
+def half_shared(meta, mine, got, out):
     count = got.shape[0]
     at = pl.ds(meta[1] * (count // 2), count // 2)
     out[: count // 2] = (mine[at].astype(F32) + got[at].astype(F32)).astype(BF)
@@ -828,9 +835,11 @@
     count = shared.shape[2]
     for j in range(cfg.lo):
         if halves:
-            own[j ^ flip] = own_in[j][...]
-            shared[wa, j ^ flip] = own_in[j][:count]
-            shared[1 - wa, j ^ flip] = other_in[j]
+            if any(which == 1 for which, _, _ in plan):
+                own[j ^ flip] = own_in[j][...]
+            if any(which == 0 for which, _, _ in plan):
+                shared[wa, j ^ flip] = own_in[j][:count]
+                shared[1 - wa, j ^ flip] = other_in[j]
             continue
         for r in range(2):
             at = 2 * (j ^ flip) + (r ^ ((meta[0] // cfg.lo) % 2))
@@ -840,11 +849,13 @@
     select = slot_select(cfg, meta)
 
     def write(out, values, transposed, at):
-        full = mm(select, values)
+        width = values.shape[1]
         if transposed:
-            out[at : at + full.shape[1], :] = full.T
+            out[at : at + width, :] = lax.dot_general(
+                values, select, (((0,), (1,)), ((), ())), preferred_element_type=F32
+            )
         else:
-            out[:, at : at + full.shape[1]] = full
+            out[:, at : at + width] = mm(select, values)
 
     for (which, i, transposed), out in zip(plan, outs):
         spots = units.places(which)[i]
@@ -951,6 +962,7 @@
         us=3,
         name="query",
         lists=1,
+        large=True,
     )
     q_send, (qraw, side_q, items) = second[:G], second[G:]
     listed = (*meta, items)
@@ -991,10 +1003,10 @@
     units_f = Units(cfg, 2 * lo, [D] * 3, [cfg.F] * 3)
     ffn = ffn_call(
         cfg, units_f, meta, x, opart, swap_cores(opart), out_adapt_out, gain_f, gate_weight, up_weight,
-        down_weight, gate_adapt_out, up_adapt_out, gate_adapt_in, up_adapt_in, down_adapt_in,
+        gate_adapt_out, up_adapt_out, gate_adapt_in, up_adapt_in, down_adapt_in,
         cot, grad_hidden, gst,
     )
-    mixed, dfn, dpart, oside, *parts_f = ffn
+    mixed, dfn, hidden, dside, oside, *parts_f = ffn
     dfn, *q_plane = after(dfn, *q_plane)
     mg = call(
         functools.partial(mixed_grad_kernel, cfg),
@@ -1074,11 +1086,14 @@
         us=0.01,
         name="sum_shared",
     )
-    shared_f, qpart, *dkv = after(shared_f, qpart, *dkv)
-    kv_grads, kv_sides, akeep_kv, asend_kv = call(
+    shared_f, qpart, *dkv = after(swap_cores(shared_f), qpart, *dkv)
+    kv_grads, kv_sides, akeep_kv, asend_kv, sum_f = call(
         functools.partial(key_value_side_kernel, cfg),
-        [((2, T, KW), BF), ((2, T, AW), BF), ((2 * S, D // 2), BF), ((2 * S, D // 2), BF)],
-        [meta] + dkv + [normed, kraw, cos, sin, kg, key_adapt_out, value_adapt_out],
+        [((2, T, KW), BF), ((2, T, AW), BF), ((2 * S, D // 2), BF), ((2 * S, D // 2), BF)]
+        + [((units_f.u - units_f.us // 2, 16, 128), BF)],
+        [meta]
+        + dkv
+        + [normed, kraw, cos, sin, kg, key_adapt_out, value_adapt_out, sum_f, shared_f],
         scratch=[pltpu.VMEM((T, 2 * KW), BF), pltpu.VMEM((2 * S, D), F32)],
         us=0.01,
         name="key_value_side",
@@ -1092,9 +1107,12 @@
         name="key_value_back",
     )
 
-    def expand(units, chunks, plan, halves, outs, name):
+    def other_core(units, chunks, halves):
         shared = units.us if halves else units.us // 2
-        theirs = swap_cores(jnp.stack([chunk[..., :shared, :, :] for chunk in chunks]))
+        return swap_cores(jnp.stack([chunk[..., :shared, :, :] for chunk in chunks]))
+
+    def expand(units, chunks, theirs, plan, halves, outs, name):
+        shared = units.us if halves else units.us // 2
         per = chunks[0].shape[-3]
         return call(
             functools.partial(expand_kernel, cfg, units, plan, halves),
@@ -1118,18 +1136,18 @@
         us=0.01,
         name="pack_qkv",
     )
-    (sum_f,) = call(
-        half_shared_kernel,
-        [((units_f.u - units_f.us // 2, 16, 128), BF)],
-        [meta, sum_f, swap_cores(shared_f)],
-        us=0.01,
-        name="half_shared",
-    )
-    sum_f, dnormed, *parts_q = after(sum_f, dnormed, *parts_q)
+    dnormed, hidden, *parts_q = after(dnormed, hidden, *parts_q)
+    (dpart,) = call(
+        functools.partial(down_kernel, cfg),
+        [((T, D + AW), BF)],
+        [meta, hidden, down_weight, dside],
+        us=3,
+        name="down_proj",
+    )
     dn_other = swap_cores(dnormed)
     near_f = permute(cfg, sum_f, near)
     sum_q = add([parts_q[0]] + [permute(cfg, parts_q[j], j) for j in range(1, lo)])
-    sum_q, dn_other, sum_f, near_f = after(sum_q, dn_other, sum_f, near_f)
+    sum_q, dn_other, dpart, sum_f, near_f = after(sum_q, dn_other, dpart, sum_f, near_f)
     all_f = to_plane(jnp.stack([sum_f, near_f]))
     (input_rows,) = call(
         functools.partial(input_grad_kernel, cfg),
@@ -1153,6 +1171,7 @@
     gate_in, up_in, down_out, gate_out, up_out, down_in = expand(
         units_f,
         all_f,
+        other_core(units_f, all_f, False),
         [(0, 0, True), (0, 1, True), (0, 2, False), (1, 0, False), (1, 1, False), (1, 2, True)],
         False,
         [((D, AW), F32), ((D, AW), F32), ((AW, D), F32)]
@@ -1160,14 +1179,24 @@
         "expand_ffn",
     )
     down_out, out_rows, *pieces_q = after(down_out, out_rows, *pieces_q)
-    query_in, key_in, value_in, out_out, out_in, query_out, key_out, value_out = expand(
+    theirs_q = other_core(units_q, pieces_q, True)
+    out_in, query_out, key_out, value_out = expand(
         units_q,
         pieces_q,
-        [(0, 0, True), (0, 1, True), (0, 2, True), (0, 3, False)]
-        + [(1, 0, True), (1, 1, False), (1, 2, False), (1, 3, False)],
+        parts_q[0].reshape(1, units_q.u, 16, 128),
+        [(1, 0, True), (1, 1, False), (1, 2, False), (1, 3, False)],
         True,
-        [((D, AW), F32)] * 3
-        + [((AW, D), F32), ((QW, AW), F32), ((AW, QW), F32), ((AW, KW), F32), ((AW, KW), F32)],
+        [((QW, AW), F32), ((AW, QW), F32), ((AW, KW), F32), ((AW, KW), F32)],
+        "expand_own",
+    )
+    theirs_q, out_in = after(theirs_q, out_in)
+    query_in, key_in, value_in, out_out = expand(
+        units_q,
+        pieces_q,
+        theirs_q,
+        [(0, 0, True), (0, 1, True), (0, 2, True), (0, 3, False)],
+        True,
+        [((D, AW), F32)] * 3 + [((AW, D), F32)],
         "expand_qkv",
     )
     return (

time: 166 us -> 165 us (level)
  Pallas kernels: 70.5 us -> 73.5 us
  local copies, waits for them, and re-layouts: 3.09 us -> 0.3 us
    pallas_call x21 -> x22, Pallas kernels: 70.5 us -> 73.5 us  [call(): pl.pallas_call(with_meta(kernel, count), out_shape=[jax.ShapeDtypeStruct(...]
    unnamed x80 -> x82, local copies, waits for them, and re-layouts: 3.04 us -> 0.25 us
  transfers between devices with their start and end apart: 53 -> 53, of which waited for: 17 -> 16; matrix products, arithmetic and copies ran while one was open for 0% -> 0% of each run, Pallas kernels for 32% -> 34%
where the time goes in v1:
time: 165 us
  Pallas kernels  73.5 us (45%)
  starting transfers between devices  56.6 us (34%)
  waiting for transfers between devices  32.3 us (20%)
    pallas_call x22, Pallas kernels, call(): pl.pallas_call(with_meta(kernel, count), out_shape=[jax.ShapeDtypeStruct(...  73.5 us
    ppermute x44, starting transfers between devices, permute(): return lax.ppermute(value, 'ctx', [(i, i ^ bits) for i in range(cfg.n)])  55.2 us
    ppermute x44, waiting for transfers between devices, permute(): return lax.ppermute(value, 'ctx', [(i, i ^ bits) for i in range(cfg.n)])  32.2 us
  transfers between devices with their start and end apart: 53, of which 16 were waited for; matrix products, arithmetic and copies ran while one was open for 0% of the time, Pallas kernels for 34%

profile of v1, /device:TPU:0, one launch (start us, length us, event | category | flops | bytes accessed | tf_op | source)
XLA Modules:
  0.0 164.6 jit_solution(1955084232213478637)
XLA Ops:
  0.6 4.6 %key_value.1 = (bf16[256,128]{1,0:T(8,128)(2,1)}, bf16[256,128]{1,0:T(8,128)(2,1)}, bf16[256,128]{1,0:T(8,128)(2,1)}, bf16[256,128]{1,0:T(8,128)(2,1)}, f32[256,...) custom-call(s32[4]{0:T(128)} %refs_0_.43, ...), custom_call_target="tpu_custom_call" | custom-call | flops 4600000000 | tf_op jit(solution)/shard_map/key_value/pallas_call | solution.py:161
  5.2 3.1 %collective-permute-start = (bf16[256,128]{1,0:T(8,128)(2,1)}, bf16[256,128]{1,0:T(8,128)(2,1)S(1)}, u32[]{:S(2)}, u32[]{:S(2)}) collective-permute-start(bf16[256,128]{1,0:T(8,128)(2,1)} %get-tuple-element.179), channel_id=1, source_target_pairs={{0,8},{2,10},{4,12},{6,14},{8,0},{10,2},{12,4},{14,6},{16,24},{18,... | collective-permute-start | bytes 196616 | tf_op jit(solution)/shard_map/ppermute | solution.py:891
  8.3 2.6 %collective-permute-start.1 = (bf16[256,128]{1,0:T(8,128)(2,1)}, bf16[256,128]{1,0:T(8,128)(2,1)S(1)}, u32[]{:S(2)}, u32[]{:S(2)}) collective-permute-start(bf16[256,128]{1,0:T(8,128)(2,1)} %get-tuple-element.180), channel_id=1, source_target_pairs={{0,16},{2,18},{4,20},{6,22},{8,24},{10,26},{12,28},{14,30},{16,0},... | collective-permute-start | bytes 196616 | tf_op jit(solution)/shard_map/ppermute | solution.py:891
  11.0 4.1 %query.1 = (bf16[256,128]{1,0:T(8,128)(2,1)}, bf16[256,128]{1,0:T(8,128)(2,1)}, bf16[256,128]{1,0:T(8,128)(2,1)}, bf16[256,128]{1,0:T(8,128)(2,1)}, f32[256,512]...) custom-call(s32[4]{0:T(128)} %refs_0_.43, s32[4]{0:T(128)} %refs_1_.43, ...), custom_call_target="tpu_custom_call" | custom-call | flops 3449999872 | tf_op jit(solution)/shard_map/query/pallas_call | solution.py:161
  20.8 2.4 %collective-permute-start.7 = (bf16[256,128]{1,0:T(8,128)(2,1)}, bf16[256,128]{1,0:T(8,128)(2,1)S(1)}, u32[]{:S(2)}, u32[]{:S(2)}) collective-permute-start(bf16[256,128]{1,0:T(8,128)(2,1)} %get-tuple-element.192), channel_id=1, source_target_pairs={{0,16},{2,18},{4,20},{6,22},{8,24},{10,26},{12,28},{14,30},{16,0},... | collective-permute-start | bytes 196616 | tf_op jit(solution)/shard_map/ppermute | solution.py:891
  23.2 2.0 %collective-permute-start.8 = (bf16[256,128]{1,0:T(8,128)(2,1)}, bf16[256,128]{1,0:T(8,128)(2,1)S(1)}, u32[]{:S(2)}, u32[]{:S(2)}) collective-permute-start(bf16[256,128]{1,0:T(8,128)(2,1)} %get-tuple-element.193), channel_id=1, source_target_pairs={{0,24},{2,26},{4,28},{6,30},{8,16},{10,18},{12,20},{14,22},{16,8},... | collective-permute-start | bytes 196616 | tf_op jit(solution)/shard_map/ppermute | solution.py:891
  25.3 3.1 %hidden_grad.1 = (f32[256,2304]{1,0:T(8,128)S(1)}, bf16[64,256]{1,0:T(8,128)(2,1)S(1)}) custom-call(s32[4]{0:T(128)S(1)} %copy-done.23, s32[4]{0:T(128)S(1)} %copy-done.24, bf16[256,1024]{1,0:T(8,128)(2,1)S(1)} %bitcast.38, bf16[2304,1024]{1,0:T(8,128)(2,1)S(1)} %copy-done.29, bf16[128,1024]{1,0:T(8,128)(2,1)S(1)} %copy-done.15, bf16[2304,128]{1,0:T(8,128)(2,1)S(1)} %copy-done.32), custom_call_target="tpu_custom_call" | custom-call | flops 3449999872 | tf_op jit(solution)/shard_map/hidden_grad/pallas_call | solution.py:161
  31.0 7.0 %attend.1 = (bf16[256,128]{1,0:T(8,128)(2,1)S(1)}, bf16[256,128]{1,0:T(8,128)(2,1)S(1)}, bf16[256,128]{1,0:T(8,128)(2,1)S(1)}, bf16[256,128]{1,0:T(8,128)(2,1)S(...) custom-call(s32[4]{0:T(128)S(1)} %copy-done.23, s32[4]{0:T(128)S(1)} %copy-done.24, ...), custom_call_target="tpu_custom_call" | custom-call | flops 13799999488 | tf_op jit(solution)/shard_map/attend/pallas_call | solution.py:161
  39.4 2.0 %collective-permute-start.10 = (bf16[256,128]{1,0:T(8,128)(2,1)S(1)}, bf16[256,128]{1,0:T(8,128)(2,1)S(1)}, u32[]{:S(2)}, u32[]{:S(2)}) collective-permute-start(bf16[256,128]{1,0:T(8,128)(2,1)S(1)} %get-tuple-element.204), channel_id=1, source_target_pairs={{0,16},{2,18},{4,20},{6,22},{8,24},{10,26},{12,28},{14,30},{16,0},... | collective-permute-start | bytes 196616 | tf_op jit(solution)/shard_map/ppermute | solution.py:891
  42.4 2.8 %collective-permute-done.10.refs_4_.refs_9_ = bf16[256,128]{1,0:T(8,128)(2,1)S(1)} collective-permute-done((bf16[256,128]{1,0:T(8,128)(2,1)S(1)}, bf16[256,128]{1,0:T(8,128)(2,1)S(1)}, u32[]{:S(2)}, u32[]{:S(2)}) %collective-permute-start.10) | collective-permute-done | bytes 65568 | tf_op jit(solution)/shard_map/ppermute | solution.py:891
  45.3 2.2 %collective-permute-done.11.refs_5_.refs_10_ = bf16[256,128]{1,0:T(8,128)(2,1)S(1)} collective-permute-done((bf16[256,128]{1,0:T(8,128)(2,1)S(1)}, bf16[256,128]{1,0:T(8,128)(2,1)S(1)}, u32[]{:S(2)}, u32[]{:S(2)}) %collective-permute-start.11) | collective-permute-done | bytes 65568 | tf_op jit(solution)/shard_map/ppermute | solution.py:891
  52.4 10.8 %ffn.1 = (f32[256,1024]{1,0:T(8,128)S(1)}, bf16[256,1024]{1,0:T(8,128)(2,1)S(1)}, bf16[256,2304]{1,0:T(8,128)(2,1)S(1)}, bf16[256,128]{1,0:T(8,128)(2,1)S(1)}, b...) custom-call(s32[4]{0:T(128)S(1)} %copy-done.23, ...), custom_call_target="tpu_custom_call" | custom-call | flops 16099999744 | tf_op jit(solution)/shard_map/ffn/pallas_call | solution.py:161
  67.6 2.0 %mixed_grad.1 = (f32[256,1024]{1,0:T(8,128)S(1)}, bf16[2,64,512]{2,1,0:T(8,128)(2,1)S(1)}, bf16[256,128]{1,0:T(8,128)(2,1)S(1)}, bf16[256,128]{1,0:T(8,128)(2,1)...) custom-call(s32[4]{0:T(128)S(1)} %copy-done.23, s32[4]{0:T(128)S(1)} %copy-done.24, ...), custom_call_target="tpu_custom_call" | custom-call | flops 11500000 | tf_op jit(solution)/shard_map/mixed_grad/pallas_call | solution.py:161
  71.3 3.1 %collective-permute-done.17.refs_3_ = bf16[256,128]{1,0:T(8,128)(2,1)S(1)} collective-permute-done((bf16[256,128]{1,0:T(8,128)(2,1)S(1)}, bf16[256,128]{1,0:T(8,128)(2,1)S(1)}, u32[]{:S(2)}, u32[]{:S(2)}) %collective-permute-start.17) | collective-permute-done | bytes 65568 | tf_op jit(solution)/shard_map/ppermute | solution.py:891
  76.6 3.9 %collective-permute-done.19.refs_5_ = bf16[256,128]{1,0:T(8,128)(2,1)S(1)} collective-permute-done((bf16[256,128]{1,0:T(8,128)(2,1)S(1)}, bf16[256,128]{1,0:T(8,128)(2,1)S(1)}, u32[]{:S(2)}, u32[]{:S(2)}) %collective-permute-start.19) | collective-permute-done | bytes 65568 | tf_op jit(solution)/shard_map/ppermute | solution.py:891
  85.8 9.3 %grad_query.1 = (bf16[256,128]{1,0:T(8,128)(2,1)S(1)}, bf16[256,128]{1,0:T(8,128)(2,1)S(1)}, bf16[256,128]{1,0:T(8,128)(2,1)S(1)}, bf16[256,128]{1,0:T(8,128)(2,1)S(1)}) custom-call(s32[4]{0:T(128)S(1)} %copy-done.23, s32[4]{0:T(128)S(1)} %copy-done.24, s32[2,47]{1,0:T(2,128)S(1)} %copy-done.35, bf16[256,128]{1,0:T(8,128)(2,1)S(1)} %copy-done.20, ...), custom_call_target="tpu_custom_call" | custom-call | flops 15525000192 | tf_op jit(solution)/shard_map/grad_query/pallas_call | solution.py:161
  98.1 2.2 %collective-permute-start.26 = (bf16[256,128]{1,0:T(8,128)(2,1)S(1)}, bf16[256,128]{1,0:T(8,128)(2,1)S(1)}, u32[]{:S(2)}, u32[]{:S(2)}) collective-permute-start(bf16[256,128]{1,0:T(8,128)(2,1)S(1)} %get-tuple-element.237), channel_id=1, source_target_pairs={{0,16},{2,18},{4,20},{6,22},{8,24},{10,26},{12,28},{14,30},{16,0},... | collective-permute-start | bytes 196616 | tf_op jit(solution)/shard_map/ppermute | solution.py:891
  101.3 10.5 %grad_key.1 = (bf16[256,128]{1,0:T(8,128)(2,1)S(1)}, bf16[256,128]{1,0:T(8,128)(2,1)S(1)}, bf16[256,128]{1,0:T(8,128)(2,1)S(1)}, bf16[256,128]{1,0:T(8,128)(2,1)S(1)}) custom-call(s32[4]{0:T(128)S(1)} %copy-done.23, s32[4]{0:T(128)S(1)} %copy-done.24, s32[2,47]{1,0:T(2,128)S(1)} %copy-done.35, bf16[4,256,128]{2,1,0:T(8,128)(2,1)S(1)} %pad_maximum_fusion.1.refs_7_.refs_3_, ...), custom_call_target="tpu_custom_call" | custom-call | flops 18400000000 | tf_op jit(solution)/shard_map/grad_key/pallas_call | solution.py:161
  112.3 3.1 %collective-permute-start.33 = (bf16[256,128]{1,0:T(8,128)(2,1)S(1)}, bf16[256,128]{1,0:T(8,128)(2,1)S(1)}, u32[]{:S(2)}, u32[]{:S(2)}) collective-permute-start(bf16[256,128]{1,0:T(8,128)(2,1)S(1)} %get-tuple-element.259), channel_id=1, source_target_pairs={{0,16},{2,18},{4,20},{6,22},{8,24},{10,26},{12,28},{14,30},{16,0},... | collective-permute-start | bytes 196616 | tf_op jit(solution)/shard_map/ppermute | solution.py:891
  116.4 2.2 %query_back.1 = (f32[256,1024]{1,0:T(8,128)S(1)}, bf16[64,512]{1,0:T(8,128)(2,1)S(1)}, bf16[64,512]{1,0:T(8,128)(2,1)S(1)}, bf16[64,512]{1,0:T(8,128)(2,1)S(1)}) custom-call(s32[4]{0:T(128)S(1)} %copy-done.23, s32[4]{0:T(128)S(1)} %copy-done.24, bf16[256,128]{1,0:T(8,128)(2,1)S(1)} %get-tuple-element.247.refs_2_, ...), custom_call_target="tpu_custom_call" | custom-call | flops 11500000 | tf_op jit(solution)/shard_map/query_back/pallas_call | solution.py:161
  119.3 2.1 %collective-permute-done.34.refs_5_ = bf16[256,128]{1,0:T(8,128)(2,1)S(1)} collective-permute-done((bf16[256,128]{1,0:T(8,128)(2,1)S(1)}, bf16[256,128]{1,0:T(8,128)(2,1)S(1)}, u32[]{:S(2)}, u32[]{:S(2)}) %collective-permute-start.34) | collective-permute-done | bytes 65568 | tf_op jit(solution)/shard_map/ppermute | solution.py:891
  121.4 2.0 %key_value_side.1 = (bf16[2,256,256]{2,1,0:T(8,128)(2,1)S(1)}, bf16[2,256,128]{2,1,0:T(8,128)(2,1)S(1)}, bf16[128,512]{1,0:T(8,128)(2,1)S(1)}, bf16[128,512]{1,0:T(8,128)(2,1)S(1)}, bf16[33,16,128]{2,1,0:T(8,128)(2,1)S(1)}) custom-call(s32[4]{0:T(128)S(1)} %copy-done.23, s32[4]{0:T(128)S(1)} %copy-done.24, bf16[256,128]{1,0:T(8,128)(2,1)S(1)} %get-tuple-element.261.refs_2_, ...), custom_call_target="tpu_custom_call" | custom-call | flops 11500000 | tf_op jit(solution)/shard_map/key_value_side/pallas_call | solution.py:161
  126.1 1.8 %collective-permute-start.39 = (bf16[28,16,128]{2,1,0:T(8,128)(2,1)S(1)}, bf16[28,16,128]{2,1,0:T(8,128)(2,1)S(1)}, u32[]{:S(2)}, u32[]{:S(2)}) collective-permute-start(bf16[28,16,128]{2,1,0:T(8,128)(2,1)S(1)} %get-tuple-element.288), channel_id=1, source_target_pairs={{0,6},{2,4},{4,2},{6,0},{8,14},{10,12},{12,10},{14,8},{16,22},{18,... | collective-permute-start | bytes 344072 | tf_op jit(solution)/shard_map/ppermute | solution.py:891
  129.7 2.0 %down_proj.1.refs_3_ = bf16[256,1152]{1,0:T(8,128)(2,1)S(1)} custom-call(s32[4]{0:T(128)S(1)} %copy-done.23, s32[4]{0:T(128)S(1)} %copy-done.24, bf16[256,2304]{1,0:T(8,128)(2,1)S(1)} %get-tuple-element.290.refs_2_, bf16[2304,1024]{1,0:T(8,128)(2,1)S(1)} %copy-done.29, bf16[256,128]{1,0:T(8,128)(2,1)S(1)} %get-tuple-element.291.refs_4_), custom_call_target="tpu_custom_call" | custom-call | flops 3449999872 | tf_op jit(solution)/shard_map/down_proj/pallas_call | solution.py:161
  133.0 1.7 %collective-permute-done.38 = bf16[28,16,128]{2,1,0:T(8,128)(2,1)S(1)} collective-permute-done((bf16[28,16,128]{2,1,0:T(8,128)(2,1)S(1)}, bf16[28,16,128]{2,1,0:T(8,128)(2,1)S(1)}, u32[]{:S(2)}, u32[]{:S(2)}) %collective-permute-start.38) | collective-permute-done | bytes 114720 | tf_op jit(solution)/shard_map/ppermute | solution.py:891
  134.8 1.8 %collective-permute-start.42 = (bf16[28,16,128]{2,1,0:T(8,128)(2,1)S(1)}, bf16[28,16,128]{2,1,0:T(8,128)(2,1)S(1)}, u32[]{:S(2)}, u32[]{:S(2)}) collective-permute-start(bf16[28,16,128]{2,1,0:T(8,128)(2,1)S(1)} %add_convert_fusion.3), channel_id=1, source_target_pairs={{0,8},{2,10},{4,12},{6,14},{8,0},{10,2},{12,4},{14,6},{16,24},{18,... | collective-permute-start | bytes 344072 | tf_op jit(solution)/shard_map/ppermute | solution.py:891
  140.2 1.9 %input_grad.1 = bf16[256,1024]{1,0:T(8,128)(2,1)} custom-call(s32[4]{0:T(128)S(1)} %copy-done.23, s32[4]{0:T(128)S(1)} %copy-done.24, bf16[256,1024]{1,0:T(8,128)(2,1)S(1)} %bitcast.37, f32[1,1024]{1,0:T(1,128)S(1)} %bitcast.48, f32[256,1024]{1,0:T(8,128)S(1)} %get-tuple-element.294.refs_4_, bf16[256,1024]{1,0:T(8,128)(2,1)S(1)} %get-tuple-element.289.refs_5_, ...), custom_call_target="tpu_custom_call" | custom-call | flops 11500000 | tf_op jit(solution)/shard_map/input_grad/pallas_call | solution.py:161
  143.0 6.2 %collective-permute-done.43 = bf16[28,16,128]{2,1,0:T(8,128)(2,1)S(1)} collective-permute-done((bf16[28,16,128]{2,1,0:T(8,128)(2,1)S(1)}, bf16[28,16,128]{2,1,0:T(8,128)(2,1)S(1)}, u32[]{:S(2)}, u32[]{:S(2)}) %collective-permute-start.43) | collective-permute-done | bytes 114720 | tf_op jit(solution)/shard_map/ppermute | solution.py:891
  155.6 3.2 %expand_ffn.1 = (f32[1024,128]{1,0:T(8,128)}, f32[1024,128]{1,0:T(8,128)}, f32[128,1024]{1,0:T(8,128)}, f32[128,2304]{1,0:T(8,128)}, f32[128,2304]{1,0:T(8,128)}, /*index=5*/f32[2304,128]{1,0:T(8,128)}) custom-call(s32[4]{0:T(128)S(1)} %copy-done.23, s32[4]{0:T(128)S(1)} %copy-done.24, bf16[2,33,16,128]{3,2,1,0:T(8,128)(2,1)S(1)} %pad_maximum_fusion.refs_2_, ...), custom_call_target="tpu_custom_call" | custom-call | flops 4600000000 | tf_op jit(solution)/shard_map/expand_ffn/pallas_call | solution.py:161
  158.9 1.7 %output.1 = bf16[256,1024]{1,0:T(8,128)(2,1)} custom-call(s32[4]{0:T(128)S(1)} %copy-done.23, s32[4]{0:T(128)S(1)} %copy-done.24, f32[256,1024]{1,0:T(8,128)S(1)} %get-tuple-element.208.refs_2_, bf16[256,1152]{1,0:T(8,128)(2,1)S(1)} %down_proj.1.refs_3_, bf16[256,1152]{1,0:T(8,128)(2,1)S(1)} %collective-permute-done.48.refs_4_, bf16[128,1024]{1,0:T(8,128)(2,1)S(1)} %copy-done.15), custom_call_target="tpu_custom_call" | custom-call | flops 11500000 | tf_op jit(solution)/shard_map/output/pallas_call | solution.py:161
  160.7 1.7 %expand_own.1 = (f32[512,128]{1,0:T(8,128)}, f32[128,512]{1,0:T(8,128)}, f32[128,256]{1,0:T(8,128)}, f32[128,256]{1,0:T(8,128)}) custom-call(s32[4]{0:T(128)S(1)} %copy-done.23, s32[4]{0:T(128)S(1)} %copy-done.24, bf16[28,16,128]{2,1,0:T(8,128)(2,1)S(1)} %add_convert_fusion.1.refs_2_, bf16[28,16,128]{2,1,0:T(8,128)(2,1)S(1)} %collective-permute-done.49.refs_3_, ...), custom_call_target="tpu_custom_call" | custom-call | flops 4600000000 | tf_op jit(solution)/shard_map/expand_own/pallas_call | solution.py:161
  162.4 2.2 %expand_qkv.1 = (f32[1024,128]{1,0:T(8,128)}, f32[1024,128]{1,0:T(8,128)}, f32[1024,128]{1,0:T(8,128)}, f32[128,1024]{1,0:T(8,128)}) custom-call(s32[4]{0:T(128)S(1)} %copy-done.23, s32[4]{0:T(128)S(1)} %copy-done.24, bf16[28,16,128]{2,1,0:T(8,128)(2,1)S(1)} %add_convert_fusion.1.refs_2_, bf16[28,16,128]{2,1,0:T(8,128)(2,1)S(1)} %collective-permute-done.49.refs_3_, ...), custom_call_target="tpu_custom_call" | custom-call | flops 4600000000 | tf_op jit(solution)/shard_map/expand_qkv/pallas_call | solution.py:161
  (195 shorter events, 51.9 us)
Async XLA Ops:
  5.2 9.9 %collective-permute-start = (bf16[256,128]{1,0:T(8,128)(2,1)}, bf16[256,128]{1,0:T(8,128)(2,1)S(1)}, u32[]{:S(2)}, u32[]{:S(2)}) collective-permute-start(bf16[256,128]{1,0:T(8,128)(2,1)} %get-tuple-element.179), channel_id=1, source_target_pairs={{0,8},{2,10},{4,12},{6,14},{8,0},{10,2},{12,4},{14,6},{16,24},{18,... | collective-permute-start | bytes 196616 | tf_op jit(solution)/shard_map/ppermute | solution.py:891
  8.3 7.5 %collective-permute-start.1 = (bf16[256,128]{1,0:T(8,128)(2,1)}, bf16[256,128]{1,0:T(8,128)(2,1)S(1)}, u32[]{:S(2)}, u32[]{:S(2)}) collective-permute-start(bf16[256,128]{1,0:T(8,128)(2,1)} %get-tuple-element.180), channel_id=1, source_target_pairs={{0,16},{2,18},{4,20},{6,22},{8,24},{10,26},{12,28},{14,30},{16,0},... | collective-permute-start | bytes 196616 | tf_op jit(solution)/shard_map/ppermute | solution.py:891
  17.2 12.2 %collective-permute-start.3 = (bf16[4,256,128]{2,1,0:T(8,128)(2,1)S(1)}, bf16[4,256,128]{2,1,0:T(8,128)(2,1)S(1)}, u32[]{:S(2)}, u32[]{:S(2)}) collective-permute-start(bf16[4,256,128]{2,1,0:T(8,128)(2,1)S(1)} %pad_maximum_fusion.1.refs_7_.refs_3_), channel_id=1, source_target_pairs={{0,2},{2,0},{4,6},{6,4},{8,10},{10,8},{12,14},{14,12},{16,18},{18,... | collective-permute-start | bytes 786440 | tf_op jit(solution)/shard_map/ppermute | solution.py:891
  18.8 12.1 %collective-permute-start.4 = (bf16[4,256,128]{2,1,0:T(8,128)(2,1)S(1)}, bf16[4,256,128]{2,1,0:T(8,128)(2,1)S(1)}, u32[]{:S(2)}, u32[]{:S(2)}) collective-permute-start(bf16[4,256,128]{2,1,0:T(8,128)(2,1)S(1)} %pad_maximum_fusion.1.refs_7_.refs_3_), channel_id=1, source_target_pairs={{0,4},{2,6},{4,0},{6,2},{8,12},{10,14},{12,8},{14,10},{16,20},{18,... | collective-permute-start | bytes 786440 | tf_op jit(solution)/shard_map/ppermute | solution.py:891
  20.3 10.6 %collective-permute-start.5 = (bf16[4,256,128]{2,1,0:T(8,128)(2,1)S(1)}, bf16[4,256,128]{2,1,0:T(8,128)(2,1)S(1)}, u32[]{:S(2)}, u32[]{:S(2)}) collective-permute-start(bf16[4,256,128]{2,1,0:T(8,128)(2,1)S(1)} %pad_maximum_fusion.1.refs_7_.refs_3_), channel_id=1, source_target_pairs={{0,6},{2,4},{4,2},{6,0},{8,14},{10,12},{12,10},{14,8},{16,22},{18,... | collective-permute-start | bytes 786440 | tf_op jit(solution)/shard_map/ppermute | solution.py:891
  20.8 7.6 %collective-permute-start.7 = (bf16[256,128]{1,0:T(8,128)(2,1)}, bf16[256,128]{1,0:T(8,128)(2,1)S(1)}, u32[]{:S(2)}, u32[]{:S(2)}) collective-permute-start(bf16[256,128]{1,0:T(8,128)(2,1)} %get-tuple-element.192), channel_id=1, source_target_pairs={{0,16},{2,18},{4,20},{6,22},{8,24},{10,26},{12,28},{14,30},{16,0},... | collective-permute-start | bytes 196616 | tf_op jit(solution)/shard_map/ppermute | solution.py:891
  48.8 14.5 %collective-permute-start.13 = (bf16[4,256,128]{2,1,0:T(8,128)(2,1)S(1)}, bf16[4,256,128]{2,1,0:T(8,128)(2,1)S(1)}, u32[]{:S(2)}, u32[]{:S(2)}) collective-permute-start(bf16[4,256,128]{2,1,0:T(8,128)(2,1)S(1)} %pad_maximum_fusion.2.refs_4_), channel_id=1, source_target_pairs={{0,2},{2,0},{4,6},{6,4},{8,10},{10,8},{12,14},{14,12},{16,18},{18,... | collective-permute-start | bytes 786440 | tf_op jit(solution)/shard_map/ppermute | solution.py:891
  50.1 13.2 %collective-permute-start.14 = (bf16[4,256,128]{2,1,0:T(8,128)(2,1)S(1)}, bf16[4,256,128]{2,1,0:T(8,128)(2,1)S(1)}, u32[]{:S(2)}, u32[]{:S(2)}) collective-permute-start(bf16[4,256,128]{2,1,0:T(8,128)(2,1)S(1)} %pad_maximum_fusion.2.refs_4_), channel_id=1, source_target_pairs={{0,4},{2,6},{4,0},{6,2},{8,12},{10,14},{12,8},{14,10},{16,20},{18,... | collective-permute-start | bytes 786440 | tf_op jit(solution)/shard_map/ppermute | solution.py:891
  50.9 13.2 %collective-permute-start.15 = (bf16[4,256,128]{2,1,0:T(8,128)(2,1)S(1)}, bf16[4,256,128]{2,1,0:T(8,128)(2,1)S(1)}, u32[]{:S(2)}, u32[]{:S(2)}) collective-permute-start(bf16[4,256,128]{2,1,0:T(8,128)(2,1)S(1)} %pad_maximum_fusion.2.refs_4_), channel_id=1, source_target_pairs={{0,6},{2,4},{4,2},{6,0},{8,14},{10,12},{12,10},{14,8},{16,22},{18,... | collective-permute-start | bytes 786440 | tf_op jit(solution)/shard_map/ppermute | solution.py:891
  64.1 17.3 %collective-permute-start.20 = (bf16[2,39,16,128]{3,2,1,0:T(8,128)(2,1)S(1)}, bf16[2,39,16,128]{3,2,1,0:T(8,128)(2,1)S(1)}, u32[]{:S(2)}, u32[]{:S(2)}) collective-permute-start(bf16[2,39,16,128]{3,2,1,0:T(8,128)(2,1)S(1)} %get-tuple-element.220), channel_id=1, source_target_pairs={{0,2},{2,0},{4,6},{6,4},{8,10},{10,8},{12,14},{14,12},{16,18},{18,... | collective-permute-start | bytes 958472 | tf_op jit(solution)/shard_map/ppermute | solution.py:891
  64.9 16.5 %collective-permute-start.21 = (bf16[2,39,16,128]{3,2,1,0:T(8,128)(2,1)S(1)}, bf16[2,39,16,128]{3,2,1,0:T(8,128)(2,1)S(1)}, u32[]{:S(2)}, u32[]{:S(2)}) collective-permute-start(bf16[2,39,16,128]{3,2,1,0:T(8,128)(2,1)S(1)} %get-tuple-element.221), channel_id=1, source_target_pairs={{0,4},{2,6},{4,0},{6,2},{8,12},{10,14},{12,8},{14,10},{16,20},{18,... | collective-permute-start | bytes 958472 | tf_op jit(solution)/shard_map/ppermute | solution.py:891
  66.4 15.0 %collective-permute-start.22 = (bf16[2,39,16,128]{3,2,1,0:T(8,128)(2,1)S(1)}, bf16[2,39,16,128]{3,2,1,0:T(8,128)(2,1)S(1)}, u32[]{:S(2)}, u32[]{:S(2)}) collective-permute-start(bf16[2,39,16,128]{3,2,1,0:T(8,128)(2,1)S(1)} %get-tuple-element.222), channel_id=1, source_target_pairs={{0,6},{2,4},{4,2},{6,0},{8,14},{10,12},{12,10},{14,8},{16,22},{18,... | collective-permute-start | bytes 958472 | tf_op jit(solution)/shard_map/ppermute | solution.py:891
  69.7 6.9 %collective-permute-start.18 = (bf16[256,128]{1,0:T(8,128)(2,1)S(1)}, bf16[256,128]{1,0:T(8,128)(2,1)S(1)}, u32[]{:S(2)}, u32[]{:S(2)}) collective-permute-start(bf16[256,128]{1,0:T(8,128)(2,1)S(1)} %get-tuple-element.215), channel_id=1, source_target_pairs={{0,16},{2,18},{4,20},{6,22},{8,24},{10,26},{12,28},{14,30},{16,0},... | collective-permute-start | bytes 196616 | tf_op jit(solution)/shard_map/ppermute | solution.py:891
  81.5 16.6 %collective-permute-start.28 = (bf16[1056,128]{1,0:T(8,128)(2,1)S(1)}, bf16[1056,128]{1,0:T(8,128)(2,1)S(1)}, u32[]{:S(2)}, u32[]{:S(2)}) collective-permute-start(bf16[1056,128]{1,0:T(8,128)(2,1)S(1)} %scale.1.refs_11_.refs_8_), channel_id=1, source_target_pairs={{0,2},{2,0},{4,6},{6,4},{8,10},{10,8},{12,14},{14,12},{16,18},{18,... | collective-permute-start | bytes 811016 | tf_op jit(solution)/shard_map/ppermute | solution.py:891
  82.7 17.6 %collective-permute-start.29 = (bf16[1056,128]{1,0:T(8,128)(2,1)S(1)}, bf16[1056,128]{1,0:T(8,128)(2,1)S(1)}, u32[]{:S(2)}, u32[]{:S(2)}) collective-permute-start(bf16[1056,128]{1,0:T(8,128)(2,1)S(1)} %scale.1.refs_11_.refs_8_), channel_id=1, source_target_pairs={{0,4},{2,6},{4,0},{6,2},{8,12},{10,14},{12,8},{14,10},{16,20},{18,... | collective-permute-start | bytes 811016 | tf_op jit(solution)/shard_map/ppermute | solution.py:891
  83.8 17.4 %collective-permute-start.30 = (bf16[1056,128]{1,0:T(8,128)(2,1)S(1)}, bf16[1056,128]{1,0:T(8,128)(2,1)S(1)}, u32[]{:S(2)}, u32[]{:S(2)}) collective-permute-start(bf16[1056,128]{1,0:T(8,128)(2,1)S(1)} %scale.1.refs_11_.refs_8_), channel_id=1, source_target_pairs={{0,6},{2,4},{4,2},{6,0},{8,14},{10,12},{12,10},{14,8},{16,22},{18,... | collective-permute-start | bytes 811016 | tf_op jit(solution)/shard_map/ppermute | solution.py:891
  85.8 9.4 %collective-permute-start.23 = (bf16[39,16,128]{2,1,0:T(8,128)(2,1)S(1)}, bf16[39,16,128]{2,1,0:T(8,128)(2,1)S(1)}, u32[]{:S(2)}, u32[]{:S(2)}) collective-permute-start(bf16[39,16,128]{2,1,0:T(8,128)(2,1)S(1)} %get-tuple-element.228), channel_id=1, source_target_pairs={{0,8},{2,10},{4,12},{6,14},{8,0},{10,2},{12,4},{14,6},{16,24},{18,... | collective-permute-start | bytes 479240 | tf_op jit(solution)/shard_map/ppermute | solution.py:891
  95.3 23.3 %collective-permute-start.24 = (bf16[39,16,128]{2,1,0:T(8,128)(2,1)S(1)}, bf16[39,16,128]{2,1,0:T(8,128)(2,1)S(1)}, u32[]{:S(2)}, u32[]{:S(2)}) collective-permute-start(bf16[39,16,128]{2,1,0:T(8,128)(2,1)S(1)} %add_convert_fusion.refs_2_), channel_id=1, source_target_pairs={{0,16},{2,18},{4,20},{6,22},{8,24},{10,26},{12,28},{14,30},{16,0},... | collective-permute-start | bytes 479240 | tf_op jit(solution)/shard_map/ppermute | solution.py:891
  96.9 15.0 %collective-permute-start.25 = (bf16[256,128]{1,0:T(8,128)(2,1)S(1)}, bf16[256,128]{1,0:T(8,128)(2,1)S(1)}, u32[]{:S(2)}, u32[]{:S(2)}) collective-permute-start(bf16[256,128]{1,0:T(8,128)(2,1)S(1)} %get-tuple-element.236), channel_id=1, source_target_pairs={{0,8},{2,10},{4,12},{6,14},{8,0},{10,2},{12,4},{14,6},{16,24},{18,... | collective-permute-start | bytes 196616 | tf_op jit(solution)/shard_map/ppermute | solution.py:891
  98.1 13.7 %collective-permute-start.26 = (bf16[256,128]{1,0:T(8,128)(2,1)S(1)}, bf16[256,128]{1,0:T(8,128)(2,1)S(1)}, u32[]{:S(2)}, u32[]{:S(2)}) collective-permute-start(bf16[256,128]{1,0:T(8,128)(2,1)S(1)} %get-tuple-element.237), channel_id=1, source_target_pairs={{0,16},{2,18},{4,20},{6,22},{8,24},{10,26},{12,28},{14,30},{16,0},... | collective-permute-start | bytes 196616 | tf_op jit(solution)/shard_map/ppermute | solution.py:891
  100.3 11.6 %collective-permute-start.27 = (bf16[256,128]{1,0:T(8,128)(2,1)S(1)}, bf16[256,128]{1,0:T(8,128)(2,1)S(1)}, u32[]{:S(2)}, u32[]{:S(2)}) collective-permute-start(bf16[256,128]{1,0:T(8,128)(2,1)S(1)} %get-tuple-element.238), channel_id=1, source_target_pairs={{0,24},{2,26},{4,28},{6,30},{8,16},{10,18},{12,20},{14,22},{16,8},... | collective-permute-start | bytes 196616 | tf_op jit(solution)/shard_map/ppermute | solution.py:891
  111.9 7.4 %collective-permute-start.32 = (bf16[256,128]{1,0:T(8,128)(2,1)S(1)}, bf16[256,128]{1,0:T(8,128)(2,1)S(1)}, u32[]{:S(2)}, u32[]{:S(2)}) collective-permute-start(bf16[256,128]{1,0:T(8,128)(2,1)S(1)} %get-tuple-element.258), channel_id=1, source_target_pairs={{0,8},{2,10},{4,12},{6,14},{8,0},{10,2},{12,4},{14,6},{16,24},{18,... | collective-permute-start | bytes 196616 | tf_op jit(solution)/shard_map/ppermute | solution.py:891
  112.3 7.0 %collective-permute-start.33 = (bf16[256,128]{1,0:T(8,128)(2,1)S(1)}, bf16[256,128]{1,0:T(8,128)(2,1)S(1)}, u32[]{:S(2)}, u32[]{:S(2)}) collective-permute-start(bf16[256,128]{1,0:T(8,128)(2,1)S(1)} %get-tuple-element.259), channel_id=1, source_target_pairs={{0,16},{2,18},{4,20},{6,22},{8,24},{10,26},{12,28},{14,30},{16,0},... | collective-permute-start | bytes 196616 | tf_op jit(solution)/shard_map/ppermute | solution.py:891
  124.0 10.7 %collective-permute-start.41 = (bf16[33,16,128]{2,1,0:T(8,128)(2,1)S(1)}, bf16[33,16,128]{2,1,0:T(8,128)(2,1)S(1)}, u32[]{:S(2)}, u32[]{:S(2)}) collective-permute-start(bf16[33,16,128]{2,1,0:T(8,128)(2,1)S(1)} %get-tuple-element.297), channel_id=1, source_target_pairs={{0,8},{2,10},{4,12},{6,14},{8,0},{10,2},{12,4},{14,6},{16,24},{18,... | collective-permute-start | bytes 405512 | tf_op jit(solution)/shard_map/ppermute | solution.py:891
  134.8 7.3 %collective-permute-start.42 = (bf16[28,16,128]{2,1,0:T(8,128)(2,1)S(1)}, bf16[28,16,128]{2,1,0:T(8,128)(2,1)S(1)}, u32[]{:S(2)}, u32[]{:S(2)}) collective-permute-start(bf16[28,16,128]{2,1,0:T(8,128)(2,1)S(1)} %add_convert_fusion.3), channel_id=1, source_target_pairs={{0,8},{2,10},{4,12},{6,14},{8,0},{10,2},{12,4},{14,6},{16,24},{18,... | collective-permute-start | bytes 344072 | tf_op jit(solution)/shard_map/ppermute | solution.py:891
  136.6 12.6 %collective-permute-start.44 = (bf16[2,33,16,128]{3,2,1,0:T(8,128)(2,1)S(1)}, bf16[2,33,16,128]{3,2,1,0:T(8,128)(2,1)S(1)}, u32[]{:S(2)}, u32[]{:S(2)}) collective-permute-start(bf16[2,33,16,128]{3,2,1,0:T(8,128)(2,1)S(1)} %pad_maximum_fusion.refs_2_), channel_id=1, source_target_pairs={{0,2},{2,0},{4,6},{6,4},{8,10},{10,8},{12,14},{14,12},{16,18},{18,... | collective-permute-start | bytes 811016 | tf_op jit(solution)/shard_map/ppermute | solution.py:891
  137.8 12.4 %collective-permute-start.45 = (bf16[2,33,16,128]{3,2,1,0:T(8,128)(2,1)S(1)}, bf16[2,33,16,128]{3,2,1,0:T(8,128)(2,1)S(1)}, u32[]{:S(2)}, u32[]{:S(2)}) collective-permute-start(bf16[2,33,16,128]{3,2,1,0:T(8,128)(2,1)S(1)} %pad_maximum_fusion.refs_2_), channel_id=1, source_target_pairs={{0,4},{2,6},{4,0},{6,2},{8,12},{10,14},{12,8},{14,10},{16,20},{18,... | collective-permute-start | bytes 811016 | tf_op jit(solution)/shard_map/ppermute | solution.py:891
  139.0 12.4 %collective-permute-start.46 = (bf16[2,33,16,128]{3,2,1,0:T(8,128)(2,1)S(1)}, bf16[2,33,16,128]{3,2,1,0:T(8,128)(2,1)S(1)}, u32[]{:S(2)}, u32[]{:S(2)}) collective-permute-start(bf16[2,33,16,128]{3,2,1,0:T(8,128)(2,1)S(1)} %pad_maximum_fusion.refs_2_), channel_id=1, source_target_pairs={{0,6},{2,4},{4,2},{6,0},{8,14},{10,12},{12,10},{14,8},{16,22},{18,... | collective-permute-start | bytes 811016 | tf_op jit(solution)/shard_map/ppermute | solution.py:891
  142.1 7.1 %collective-permute-start.43 = (bf16[28,16,128]{2,1,0:T(8,128)(2,1)S(1)}, bf16[28,16,128]{2,1,0:T(8,128)(2,1)S(1)}, u32[]{:S(2)}, u32[]{:S(2)}) collective-permute-start(bf16[28,16,128]{2,1,0:T(8,128)(2,1)S(1)} %add_convert_fusion.2), channel_id=1, source_target_pairs={{0,16},{2,18},{4,20},{6,22},{8,24},{10,26},{12,28},{14,30},{16,0},... | collective-permute-start | bytes 344072 | tf_op jit(solution)/shard_map/ppermute | solution.py:891
  151.6 7.3 %collective-permute-start.48 = (bf16[256,1152]{1,0:T(8,128)(2,1)S(1)}, bf16[256,1152]{1,0:T(8,128)(2,1)S(1)}, u32[]{:S(2)}, u32[]{:S(2)}) collective-permute-start(bf16[256,1152]{1,0:T(8,128)(2,1)S(1)} %down_proj.1.refs_3_), channel_id=1, source_target_pairs={{0,1},{1,0},{2,3},{3,2},{4,5},{5,4},{6,7},{7,6},{8,9},{9,8},{10,11... | collective-permute-start | bytes 1769480 | tf_op jit(solution)/shard_map/ppermute | solution.py:887
  152.1 8.4 %collective-permute-start.49 = (bf16[28,16,128]{2,1,0:T(8,128)(2,1)S(1)}, bf16[28,16,128]{2,1,0:T(8,128)(2,1)S(1)}, u32[]{:S(2)}, u32[]{:S(2)}) collective-permute-start(bf16[28,16,128]{2,1,0:T(8,128)(2,1)S(1)} %add_convert_fusion.1.refs_2_), channel_id=1, source_target_pairs={{0,2},{2,0},{4,6},{6,4},{8,10},{10,8},{12,14},{14,12},{16,18},{18,... | collective-permute-start | bytes 344072 | tf_op jit(solution)/shard_map/ppermute | solution.py:891
  153.0 7.5 %collective-permute-start.50 = (bf16[28,16,128]{2,1,0:T(8,128)(2,1)S(1)}, bf16[28,16,128]{2,1,0:T(8,128)(2,1)S(1)}, u32[]{:S(2)}, u32[]{:S(2)}) collective-permute-start(bf16[28,16,128]{2,1,0:T(8,128)(2,1)S(1)} %add_convert_fusion.1.refs_2_), channel_id=1, source_target_pairs={{0,4},{2,6},{4,0},{6,2},{8,12},{10,14},{12,8},{14,10},{16,20},{18,... | collective-permute-start | bytes 344072 | tf_op jit(solution)/shard_map/ppermute | solution.py:891
  (62 other events, 646.3 us)
